TPU v7x, 32 devices: a whole 2x2x4 slice. The times are simulated.
32 devices in a mesh: dp: 8 (over z, x), fsdp: 4 (over y, core).
Axes of the slice: x: 2, y: 2, z: 4, core: 2. Of those that a mesh axis runs over, the one named last changes fastest.
Arguments:
- tokens: bfloat16 [32768, 768], P(('dp', 'fsdp')), may hold values from -6 to 6
- layout_cells: int32 [2, 32768], P(None, ('dp', 'fsdp')), may hold values from 0 to 31
- pad_mask: int32 [32768], P(('dp', 'fsdp')), may hold values from 0 to 1, as said below
- query_weight: bfloat16 [768, 768], P('fsdp'), may hold values from -0.21875 to 0.21875
- key_weight: bfloat16 [768, 768], P('fsdp'), may hold values from -0.21875 to 0.21875
- value_weight: bfloat16 [768, 768], P('fsdp'), may hold values from -0.21875 to 0.21875
- out_weight: bfloat16 [768, 768], P('fsdp'), may hold values from -0.875 to 0.875
- query_bias: bfloat16 [768], P('fsdp'), may hold values from -4 to 4
- value_bias: bfloat16 [768], P('fsdp'), may hold values from -4 to 4
- out_bias: bfloat16 [768], P('fsdp'), may hold values from -4 to 4
- bias_table: bfloat16 [12, 96], P('fsdp'), may hold values from -4 to 4
- first_gain: bfloat16 [768], P('fsdp'), may hold values from 0.25 to 1.75
- first_shift: bfloat16 [768], P('fsdp'), may hold values from -4 to 4
- up_weight: bfloat16 [768, 3072], P('fsdp'), may hold values from -0.21875 to 0.21875
- up_bias: bfloat16 [3072], P('fsdp'), may hold values from -4 to 4
- down_weight: bfloat16 [3072, 768], P('fsdp'), may hold values from -0.109375 to 0.109375
- down_bias: bfloat16 [768], P('fsdp'), may hold values from -4 to 4
- second_gain: bfloat16 [768], P('fsdp'), may hold values from 0.25 to 1.75
- second_shift: bfloat16 [768], P('fsdp'), may hold values from -4 to 4
- cotangent: bfloat16 [32768, 768], P(('dp', 'fsdp')), may hold values from -6 to 6
Outputs:
- output: bfloat16 [32768, 768], P(('dp', 'fsdp'))
- input_grad: bfloat16 [32768, 768], P(('dp', 'fsdp'))
- grad_query: float32 [768, 768], P('fsdp')
- grad_key: float32 [768, 768], P('fsdp')
- grad_value: float32 [768, 768], P('fsdp')
- grad_out: float32 [768, 768], P('fsdp')
- grad_query_bias: float32 [768], P('fsdp')
- grad_value_bias: float32 [768], P('fsdp')
- grad_out_bias: float32 [768], P('fsdp')
- grad_table: float32 [12, 96], P('fsdp')
- grad_first_gain: float32 [768], P('fsdp')
- grad_first_shift: float32 [768], P('fsdp')
- grad_up: float32 [768, 3072], P('fsdp')
- grad_up_bias: float32 [3072], P('fsdp')
- grad_down: float32 [3072, 768], P('fsdp')
- grad_down_bias: float32 [768], P('fsdp')
- grad_second_gain: float32 [768], P('fsdp')
- grad_second_shift: float32 [768], P('fsdp')
Inputs may be any that keep to these rules, and one draw needn't show every extreme that they name: `pad_mask`: within each window of 512 consecutive tokens the ones form a prefix of one token or more; some windows are all ones.
All inputs are finite; a program needn't handle non-finite values.
Results may differ from a plain program's by a relative error of at most 0.017.
Values may be sent and summed in bfloat16 or wider, within the bound.
No kernel may reach another device: no remote copies, remote signals or barrier semaphores. Data moves between devices by JAX's collectives and lax.ppermute only.
A program may use at most 256 MiB of HBM per device.

v0:
```python
import math

import jax
import jax.numpy as jnp
from jax import lax
from jax.sharding import PartitionSpec as P

HEADS = 12
HD = 64
WIN = 512
BUCKETS = 32


def layer_norm(hidden, gain, shift):
    centre = hidden - jnp.mean(hidden, axis=-1, keepdims=True)
    spread = jnp.mean(centre * centre, axis=-1, keepdims=True)
    return centre * lax.rsqrt(spread + 1e-05) * gain + shift


def gelu_exact(values):
    return jax.nn.gelu(values, approximate=False)


def bucket_onehot(cell_x, cell_y):
    places = jnp.arange(WIN, dtype=jnp.int32)
    half_span = BUCKETS // 2
    labels = jnp.arange(BUCKETS, dtype=jnp.int32)
    tables = []
    for coords in (places, cell_x, cell_y):
        relative = (
            jnp.clip(coords[None, :] - coords[:, None], -half_span, half_span - 1) + half_span
        )
        tables.append(relative.reshape(1, -1) == labels[:, None])
    return jnp.concatenate(tables, axis=0).astype(jnp.bfloat16)


def window_scores(query_win, key_win, cell_x, cell_y, valid_win, table):
    onehot = bucket_onehot(cell_x, cell_y)
    rel_bias = jnp.dot(table, onehot, preferred_element_type=jnp.float32).reshape(HEADS, WIN, WIN)
    raw_scores = (
        jnp.einsum("qhd,khd->hqk", query_win, key_win, preferred_element_type=jnp.float32)
        * HD ** (-0.5)
        + rel_bias
    )
    return (jnp.where(valid_win[None, None, :], raw_scores, -1e30), onehot)


def times_transposed(left, weight):
    return lax.dot_general(
        left, weight, (((1,), (1,)), ((), ())), preferred_element_type=jnp.float32
    )


def rows_product(left, right):
    return lax.dot_general(
        left, right, (((0,), (0,)), ((), ())), preferred_element_type=jnp.float32
    )


def column_sum(values):
    return jnp.sum(values, axis=0, dtype=jnp.float32)


def on_device(
    tokens,
    layout_cells,
    pad_mask,
    query_weight,
    key_weight,
    value_weight,
    out_weight,
    query_bias,
    value_bias,
    out_bias,
    bias_table,
    first_gain,
    first_shift,
    up_weight,
    up_bias,
    down_weight,
    down_bias,
    second_gain,
    second_shift,
    cotangent,
):
    row_count = tokens.shape[0]
    windows = row_count // WIN
    full = (
        lax.all_gather(query_weight, "fsdp", axis=0, tiled=True),
        lax.all_gather(key_weight, "fsdp", axis=0, tiled=True),
        lax.all_gather(value_weight, "fsdp", axis=0, tiled=True),
        lax.all_gather(out_weight, "fsdp", axis=0, tiled=True),
        lax.all_gather(query_bias, "fsdp", axis=0, tiled=True),
        lax.all_gather(value_bias, "fsdp", axis=0, tiled=True),
        lax.all_gather(out_bias, "fsdp", axis=0, tiled=True),
        lax.all_gather(bias_table, "fsdp", axis=0, tiled=True),
        lax.all_gather(first_gain, "fsdp", axis=0, tiled=True),
        lax.all_gather(first_shift, "fsdp", axis=0, tiled=True),
        lax.all_gather(up_weight, "fsdp", axis=0, tiled=True),
        lax.all_gather(up_bias, "fsdp", axis=0, tiled=True),
        lax.all_gather(down_weight, "fsdp", axis=0, tiled=True),
        lax.all_gather(down_bias, "fsdp", axis=0, tiled=True),
        lax.all_gather(second_gain, "fsdp", axis=0, tiled=True),
        lax.all_gather(second_shift, "fsdp", axis=0, tiled=True),
    )
    (
        full_query,
        full_key,
        full_value,
        full_out,
        bias_query,
        bias_value,
        bias_out,
        full_table,
        gain_one,
        shift_one,
        full_up,
        bias_up,
        full_down,
        bias_down,
        gain_two,
        shift_two,
    ) = full

    def to_windows(array):
        return array.reshape(windows, WIN, HEADS, HD)

    queries = (
        jnp.dot(tokens, full_query, preferred_element_type=jnp.float32)
        + bias_query.astype(jnp.float32)
    ).astype(jnp.bfloat16)
    key_rows = jnp.dot(tokens, full_key, preferred_element_type=jnp.float32).astype(jnp.bfloat16)
    value_rows = (
        jnp.dot(tokens, full_value, preferred_element_type=jnp.float32)
        + bias_value.astype(jnp.float32)
    ).astype(jnp.bfloat16)
    cells_x = layout_cells[0].reshape(windows, WIN)
    cells_y = layout_cells[1].reshape(windows, WIN)
    valid_keys = pad_mask.reshape(windows, WIN) > 0

    def attend(pieces):
        query_win, key_win, value_win, cell_x, cell_y, valid_win = pieces
        scores, onehot = window_scores(query_win, key_win, cell_x, cell_y, valid_win, full_table)
        row_max = jnp.max(scores, axis=-1, keepdims=True)
        exponent = jnp.exp(scores - row_max)
        denominator = jnp.sum(exponent, axis=-1, keepdims=True)
        probability = (exponent / denominator).astype(jnp.bfloat16)
        mixed_win = jnp.einsum(
            "hqk,khd->qhd", probability, value_win, preferred_element_type=jnp.float32
        )
        return (mixed_win.astype(jnp.bfloat16), row_max[..., 0] + jnp.log(denominator[..., 0]))

    mixed_all, log_totals = lax.map(
        attend,
        (
            to_windows(queries),
            to_windows(key_rows),
            to_windows(value_rows),
            cells_x,
            cells_y,
            valid_keys,
        ),
    )
    mixed_rows = mixed_all.reshape(row_count, HEADS * HD)
    attended = jnp.dot(mixed_rows, full_out, preferred_element_type=jnp.float32) + bias_out.astype(
        jnp.float32
    )
    resid = tokens.astype(jnp.float32) + attended
    normed, first_pull = jax.vjp(
        layer_norm, resid, gain_one.astype(jnp.float32), shift_one.astype(jnp.float32)
    )
    normed_low = normed.astype(jnp.bfloat16)
    hidden = jnp.dot(normed_low, full_up, preferred_element_type=jnp.float32) + bias_up.astype(
        jnp.float32
    )
    active, gelu_pull = jax.vjp(gelu_exact, hidden)
    active_low = active.astype(jnp.bfloat16)
    final = (
        normed
        + jnp.dot(active_low, full_down, preferred_element_type=jnp.float32)
        + bias_down.astype(jnp.float32)
    )
    result, second_pull = jax.vjp(
        layer_norm, final, gain_two.astype(jnp.float32), shift_two.astype(jnp.float32)
    )
    again = (
        lax.all_gather(query_weight, "fsdp", axis=0, tiled=True),
        lax.all_gather(key_weight, "fsdp", axis=0, tiled=True),
        lax.all_gather(value_weight, "fsdp", axis=0, tiled=True),
        lax.all_gather(out_weight, "fsdp", axis=0, tiled=True),
        lax.all_gather(query_bias, "fsdp", axis=0, tiled=True),
        lax.all_gather(value_bias, "fsdp", axis=0, tiled=True),
        lax.all_gather(out_bias, "fsdp", axis=0, tiled=True),
        lax.all_gather(bias_table, "fsdp", axis=0, tiled=True),
        lax.all_gather(first_gain, "fsdp", axis=0, tiled=True),
        lax.all_gather(first_shift, "fsdp", axis=0, tiled=True),
        lax.all_gather(up_weight, "fsdp", axis=0, tiled=True),
        lax.all_gather(up_bias, "fsdp", axis=0, tiled=True),
        lax.all_gather(down_weight, "fsdp", axis=0, tiled=True),
        lax.all_gather(down_bias, "fsdp", axis=0, tiled=True),
        lax.all_gather(second_gain, "fsdp", axis=0, tiled=True),
        lax.all_gather(second_shift, "fsdp", axis=0, tiled=True),
    )
    back_query, back_key, back_value, back_out = (again[0], again[1], again[2], again[3])
    back_table, back_up, back_down = (again[7], again[10], again[12])
    dfinal, grad_gain_two, grad_shift_two = second_pull(cotangent.astype(jnp.float32))
    dbranch = dfinal.astype(jnp.bfloat16)
    grad_down = rows_product(active_low, dbranch)
    grad_down_bias = column_sum(dbranch)
    dactive = times_transposed(dbranch, back_down)
    dhidden = gelu_pull(dactive)[0].astype(jnp.bfloat16)
    grad_up = rows_product(normed_low, dhidden)
    grad_up_bias = column_sum(dhidden)
    dnormed = dfinal + times_transposed(dhidden, back_up)
    dresid, grad_gain_one, grad_shift_one = first_pull(dnormed)
    dattn = dresid.astype(jnp.bfloat16)
    grad_out = rows_product(mixed_rows, dattn)
    grad_out_bias = column_sum(dattn)
    dmixed = times_transposed(dattn, back_out).astype(jnp.bfloat16)

    def attend_back(pieces):
        query_win, key_win, value_win, dmixed_win, lse_win, cell_x, cell_y, valid_win = pieces
        scores, onehot = window_scores(query_win, key_win, cell_x, cell_y, valid_win, back_table)
        probability = jnp.exp(scores - lse_win[:, :, None])
        dvalue = jnp.einsum(
            "hqk,qhd->khd",
            probability.astype(jnp.bfloat16),
            dmixed_win,
            preferred_element_type=jnp.float32,
        )
        dprobs = jnp.einsum(
            "qhd,khd->hqk", dmixed_win, value_win, preferred_element_type=jnp.float32
        )
        dscores = (
            probability * (dprobs - jnp.sum(probability * dprobs, axis=-1, keepdims=True))
        ).astype(jnp.bfloat16)
        dquery = jnp.einsum(
            "hqk,khd->qhd", dscores, key_win, preferred_element_type=jnp.float32
        ) * HD ** (-0.5)
        dkey = jnp.einsum(
            "hqk,qhd->khd", dscores, query_win, preferred_element_type=jnp.float32
        ) * HD ** (-0.5)
        dtable = times_transposed(dscores.reshape(HEADS, WIN * WIN), onehot)
        return (
            dquery.astype(jnp.bfloat16),
            dkey.astype(jnp.bfloat16),
            dvalue.astype(jnp.bfloat16),
            dtable,
        )

    dquery_all, dkey_all, dvalue_all, dtable_all = lax.map(
        attend_back,
        (
            to_windows(queries),
            to_windows(key_rows),
            to_windows(value_rows),
            to_windows(dmixed),
            log_totals,
            cells_x,
            cells_y,
            valid_keys,
        ),
    )
    dquery_rows = dquery_all.reshape(row_count, HEADS * HD)
    dkey_rows = dkey_all.reshape(row_count, HEADS * HD)
    dvalue_rows = dvalue_all.reshape(row_count, HEADS * HD)
    grad_table = jnp.sum(dtable_all, axis=0)
    grad_query = rows_product(tokens, dquery_rows)
    grad_key = rows_product(tokens, dkey_rows)
    grad_value = rows_product(tokens, dvalue_rows)
    grad_query_bias = column_sum(dquery_rows)
    grad_value_bias = column_sum(dvalue_rows)
    input_sum = (
        dresid
        + times_transposed(dquery_rows, back_query)
        + times_transposed(dkey_rows, back_key)
        + times_transposed(dvalue_rows, back_value)
    )
    input_grad = input_sum.astype(jnp.bfloat16)
    wide = lax.axis_size("dp")
    narrow = lax.axis_size("fsdp")
    parts = (
        lax.psum_scatter(
            grad_query.astype(jnp.bfloat16), "fsdp", scatter_dimension=0, tiled=True
        ).astype(jnp.float32),
        lax.psum_scatter(
            grad_key.astype(jnp.bfloat16), "fsdp", scatter_dimension=0, tiled=True
        ).astype(jnp.float32),
        lax.psum_scatter(
            grad_value.astype(jnp.bfloat16), "fsdp", scatter_dimension=0, tiled=True
        ).astype(jnp.float32),
        lax.psum_scatter(
            grad_out.astype(jnp.bfloat16), "fsdp", scatter_dimension=0, tiled=True
        ).astype(jnp.float32),
        lax.psum_scatter(
            grad_query_bias.astype(jnp.bfloat16), "fsdp", scatter_dimension=0, tiled=True
        ).astype(jnp.float32),
        lax.psum_scatter(
            grad_value_bias.astype(jnp.bfloat16), "fsdp", scatter_dimension=0, tiled=True
        ).astype(jnp.float32),
        lax.psum_scatter(
            grad_out_bias.astype(jnp.bfloat16), "fsdp", scatter_dimension=0, tiled=True
        ).astype(jnp.float32),
        lax.psum_scatter(
            grad_table.astype(jnp.bfloat16), "fsdp", scatter_dimension=0, tiled=True
        ).astype(jnp.float32),
        lax.psum_scatter(
            grad_gain_one.astype(jnp.bfloat16), "fsdp", scatter_dimension=0, tiled=True
        ).astype(jnp.float32),
        lax.psum_scatter(
            grad_shift_one.astype(jnp.bfloat16), "fsdp", scatter_dimension=0, tiled=True
        ).astype(jnp.float32),
        lax.psum_scatter(
            grad_up.astype(jnp.bfloat16), "fsdp", scatter_dimension=0, tiled=True
        ).astype(jnp.float32),
        lax.psum_scatter(
            grad_up_bias.astype(jnp.bfloat16), "fsdp", scatter_dimension=0, tiled=True
        ).astype(jnp.float32),
        lax.psum_scatter(
            grad_down.astype(jnp.bfloat16), "fsdp", scatter_dimension=0, tiled=True
        ).astype(jnp.float32),
        lax.psum_scatter(
            grad_down_bias.astype(jnp.bfloat16), "fsdp", scatter_dimension=0, tiled=True
        ).astype(jnp.float32),
        lax.psum_scatter(
            grad_gain_two.astype(jnp.bfloat16), "fsdp", scatter_dimension=0, tiled=True
        ).astype(jnp.float32),
        lax.psum_scatter(
            grad_shift_two.astype(jnp.bfloat16), "fsdp", scatter_dimension=0, tiled=True
        ).astype(jnp.float32),
    )
    sums = lax.psum(
        (
            parts[0],
            parts[1],
            parts[2],
            parts[3],
            parts[4],
            parts[5],
            parts[6],
            parts[7],
            parts[8],
            parts[9],
            parts[10],
            parts[11],
            parts[12],
            parts[13],
            parts[14],
            parts[15],
        ),
        "dp",
    )
    factor = 1.0 / math.sqrt(row_count * wide * narrow)
    return (result.astype(jnp.bfloat16), input_grad) + tuple((total * factor for total in sums))


def solution(mesh):
    placed = (
        P(("dp", "fsdp"), None),
        P(None, ("dp", "fsdp")),
        P(("dp", "fsdp")),
        P("fsdp", None),
        P("fsdp", None),
        P("fsdp", None),
        P("fsdp", None),
        P("fsdp"),
        P("fsdp"),
        P("fsdp"),
        P("fsdp", None),
        P("fsdp"),
        P("fsdp"),
        P("fsdp", None),
        P("fsdp"),
        P("fsdp", None),
        P("fsdp"),
        P("fsdp"),
        P("fsdp"),
        P(("dp", "fsdp"), None),
    )
    return jax.shard_map(
        on_device,
        mesh=mesh,
        in_specs=placed,
        out_specs=(
            P(("dp", "fsdp"), None),
            P(("dp", "fsdp"), None),
            P("fsdp", None),
            P("fsdp", None),
            P("fsdp", None),
            P("fsdp", None),
            P("fsdp"),
            P("fsdp"),
            P("fsdp"),
            P("fsdp", None),
            P("fsdp"),
            P("fsdp"),
            P("fsdp", None),
            P("fsdp"),
            P("fsdp", None),
            P("fsdp"),
            P("fsdp"),
            P("fsdp"),
        ),
        check_vma=False,
    )
```

profile of v0, /device:TPU:0, one launch (start us, length us, event | category | flops | bytes accessed | tf_op | source)
XLA Modules:
  0.0 1270.2 jit_solution(2293533152153365275)
XLA Ops:
  14.3 13.2 %all-reduce.20 = (bf16[768]{0:T(1024)(128)(2,1)S(1)}, bf16[768]{0:T(1024)(128)(2,1)S(1)}, bf16[768]{0:T(1024)(128)(2,1)S(1)}, bf16[768]{0:T(1024)(128)(2,1)S(1)}...) all-reduce(bf16[768]{0:T(1024)(128)(2,1)S(1)} %dynamic-update-slice, ...), channel_id=1, replica_groups=mesh['dp'=8,'fsdp'=4] {'fsdp'}, use_global_device_ids=true, to_apply=%add.1 | all-reduce | flops 5376 | bytes 21504
  30.5 5.1 all-gather
  35.7 5.2 all-gather.1
  58.1 10.1 all-gather.13.cloned.1.call-done
  68.2 4.3 convolution_convert_fusion.3
  79.8 176.7 %while.28 = (s32[]{:T(128)}, bf16[2,512,12,64]{1,3,2,0:T(8,128)(2,1)}, f32[2,12,512]{2,1,0:T(8,128)S(1)}, bf16[2,512,12,64]{1,3,2,0:T(8,128)(2,1)}, pred[2,512]{...) while((s32[]{:T(128)}, ...), condition=%wide.region_3.4_spmd, body=%wide.region_0.3_spmd.sunk | while | flops 1515841536 | bytes 219408304 | solution.py:153
  81.5 5.5 iota_compare_fusion.14
  87.1 5.5 iota_compare_fusion.12
  92.6 5.4 iota_compare_fusion.13
  98.0 15.5 %fusion.157 = f32[262144,12]{0,1:T(8,128)S(1)} fusion(bf16[12,96]{1,0:T(8,128)(2,1)S(1)} %get-tuple-element.598, pred[32,262144]{1,0:T(32,128)(4,1)} %iota_compare_fusion.12, pred[32,262144]{1,0:T(32,128)(4,1)} %iota_compare_fusion.13, pred[32,262144]{1,0:T(32,128)(4,1)} %iota_compare_fusion.14), kind=kOutput, calls=%fused_computation.clone.1 | convolution fusion | flops 654311424 | bytes 37751040 | tf_op jit(solution)/shard_map/while/body/eval_jaxpr/dot_general | solution.py:39
  113.6 19.1 %copy.176 = f32[2,8,512,512]{3,2,1,0:T(8,128)} copy(f32[2,8,512,512]{3,1,2,0:T(8,128)S(1)} %bitcast.280) | data formatting | bytes 33554432 | tf_op jit(solution)/shard_map/while
  132.7 12.1 slice.14
  144.8 12.8 %copy.177 = f32[12,512,512]{1,2,0:T(8,128)} copy(f32[12,512,512]{2,1,0:T(8,128)} %slice.14) | data formatting | bytes 25165824 | tf_op jit(solution)/shard_map/while/body/eval_jaxpr/reshape | solution.py:39
  157.5 6.3 fusion.158
  170.5 5.5 iota_compare_fusion.14
  176.1 5.5 iota_compare_fusion.12
  181.6 5.4 iota_compare_fusion.13
  187.0 15.4 %fusion.157 = f32[262144,12]{0,1:T(8,128)S(1)} fusion(bf16[12,96]{1,0:T(8,128)(2,1)S(1)} %get-tuple-element.598, pred[32,262144]{1,0:T(32,128)(4,1)} %iota_compare_fusion.12, pred[32,262144]{1,0:T(32,128)(4,1)} %iota_compare_fusion.13, pred[32,262144]{1,0:T(32,128)(4,1)} %iota_compare_fusion.14), kind=kOutput, calls=%fused_computation.clone.1 | convolution fusion | flops 654311424 | bytes 37751040 | tf_op jit(solution)/shard_map/while/body/eval_jaxpr/dot_general | solution.py:39
  202.4 19.1 %copy.176 = f32[2,8,512,512]{3,2,1,0:T(8,128)} copy(f32[2,8,512,512]{3,1,2,0:T(8,128)S(1)} %bitcast.280) | data formatting | bytes 33554432 | tf_op jit(solution)/shard_map/while
  221.5 10.6 slice.14
  232.2 12.7 copy.177
  244.8 6.2 fusion.158
  267.0 38.0 %multiply_convert_fusion.3 = (bf16[1024,3072]{1,0:T(8,128)(2,1)}, f32[1024,3072]{1,0:T(8,128)}, f32[1024,3072]{1,0:T(8,128)}) fusion(f32[3072]{0:T(1024)S(1)} %bitcast.303, bf16[768,3072]{1,0:T(8,128)(2,1)} %all-gather.17.cloned.1.call-done, f32[1024,768]{0,1:T(8,128)S(1)} %get-tuple-element.390, f32[768]{0:T(1024)S(1)} %copy-done.70, ...), kind=kOutput, calls=%fused_computation.83 | convolution fusion | flops 5043388416 | bytes 39348224 | tf_op jit(solution)/shard_map/dot_general | solution.py:173
  305.0 9.7 fusion.83
  319.6 18.0 %fusion.84 = (bf16[3072]{0:T(1024)(128)(2,1)}, bf16[1024,3072]{1,0:T(8,128)(2,1)}) fusion(f32[1024,3072]{1,0:T(8,128)} %get-tuple-element.376, bf16[1024,768]{0,1:T(8,128)(2,1)S(1)} %get-tuple-element.370, bf16[3072,768]{1,0:T(8,128)(2,1)} %all-gather.19.cloned.1.call-done, f32[1024,3072]{1,0:T(8,128)} %get-tuple-element.391, f32[3072]{0:T(1024)S(1)} %bitcast.304), kind=kOutput, calls=%fused_computation.179 | convolution fusion | flops 4882166784 | bytes 37767168 | tf_op jit(solution)/shard_map/dot_general | solution.py:49
  337.7 11.8 multiply_reduce_fusion.1
  364.4 370.6 %while.29 = (s32[]{:T(128)}, bf16[2,512,12,64]{1,3,2,0:T(8,128)(2,1)}, bf16[2,512,12,64]{1,3,2,0:T(8,128)(2,1)}, bf16[2,512,12,64]{1,3,2,0:T(8,128)(2,1)}, f32[2...) while((s32[]{:T(128)}, ...), condition=%wide.region_14.15_spmd, body=%wide.region_12.14_spmd.sunk | while | flops 3332499456 | bytes 488264960 | solution.py:251
  385.7 4.8 iota_compare_fusion.17
  390.5 5.5 iota_compare_fusion.15
  396.0 5.5 iota_compare_fusion.16
  401.5 14.5 %pad_add_fusion.2 = pred[96,262144]{1,0:T(32,128)(4,1)} fusion(pred[32,262144]{1,0:T(32,128)(4,1)} %iota_compare_fusion.15, pred[32,262144]{1,0:T(32,128)(4,1)} %iota_compare_fusion.16, pred[32,262144]{1,0:T(32,128)(4,1)S(1)} %iota_compare_fusion.17), kind=kLoop, calls=%fused_computation.33.clone.1 | loop fusion | flops 50331648 | bytes 50331648 | tf_op jit(solution)/shard_map/while/body/eval_jaxpr/concatenate | solution.py:34
  416.0 7.5 fusion.173
  423.4 20.2 %fusion.174 = f32[262144,12]{0,1:T(8,128)} fusion(pred[96,262144]{1,0:T(32,128)(4,1)} %pad_add_fusion.2, bf16[12,96]{1,0:T(8,128)(2,1)S(1)} %get-tuple-element.642), kind=kOutput, calls=%fused_computation.180.clone.1 | convolution fusion | flops 603979776 | bytes 37751040 | tf_op jit(solution)/shard_map/while/body/eval_jaxpr/dot_general | solution.py:39
  443.6 17.7 %copy.181 = f32[2,8,512,512]{3,2,1,0:T(8,128)} copy(f32[2,8,512,512]{3,1,2,0:T(8,128)} %bitcast.275) | data formatting | bytes 33554432 | tf_op jit(solution)/shard_map/while
  461.3 10.7 slice.15
  471.9 12.7 copy.182
  484.6 11.1 multiply_reduce_fusion.6
  495.7 6.9 multiply_convert_fusion.5
  511.3 9.2 copy.183
  520.5 6.7 pad.35
  527.3 11.4 copy.184
  538.6 17.0 %fusion.178 = f32[2,12,96]{2,1,0:T(8,128)S(1)} fusion(f32[2,12,96]{2,1,0:T(8,128)S(1)} %get-tuple-element.620, s32[]{:T(128)S(6)} %copy.213, bf16[12,262144]{1,0:T(8,128)(2,1)} %bitcast.278, pred[96,262144]{1,0:T(32,128)(4,1)} %pad_add_fusion.2), kind=kOutput, calls=%fused_computation.52.clone.1 | convolution fusion | flops 603979776 | bytes 31465476 | tf_op jit(solution)/shard_map/while/body/eval_jaxpr/dot_general | solution.py:49
  557.3 4.8 iota_compare_fusion.17
  562.1 5.5 iota_compare_fusion.15
  567.6 5.5 iota_compare_fusion.16
  573.1 14.5 %pad_add_fusion.2 = pred[96,262144]{1,0:T(32,128)(4,1)} fusion(pred[32,262144]{1,0:T(32,128)(4,1)} %iota_compare_fusion.15, pred[32,262144]{1,0:T(32,128)(4,1)} %iota_compare_fusion.16, pred[32,262144]{1,0:T(32,128)(4,1)S(1)} %iota_compare_fusion.17), kind=kLoop, calls=%fused_computation.33.clone.1 | loop fusion | flops 50331648 | bytes 50331648 | tf_op jit(solution)/shard_map/while/body/eval_jaxpr/concatenate | solution.py:34
  587.6 7.5 fusion.173
  595.0 20.2 %fusion.174 = f32[262144,12]{0,1:T(8,128)} fusion(pred[96,262144]{1,0:T(32,128)(4,1)} %pad_add_fusion.2, bf16[12,96]{1,0:T(8,128)(2,1)S(1)} %get-tuple-element.642), kind=kOutput, calls=%fused_computation.180.clone.1 | convolution fusion | flops 603979776 | bytes 37751040 | tf_op jit(solution)/shard_map/while/body/eval_jaxpr/dot_general | solution.py:39
  615.2 17.7 %copy.181 = f32[2,8,512,512]{3,2,1,0:T(8,128)} copy(f32[2,8,512,512]{3,1,2,0:T(8,128)} %bitcast.275) | data formatting | bytes 33554432 | tf_op jit(solution)/shard_map/while
  632.9 10.7 slice.15
  643.6 12.7 copy.182
  656.2 11.1 multiply_reduce_fusion.6
  667.3 6.9 multiply_convert_fusion.5
  682.9 9.2 copy.183
  692.1 6.7 pad.35
  698.9 11.4 copy.184
  710.3 17.0 %fusion.178 = f32[2,12,96]{2,1,0:T(8,128)S(1)} fusion(f32[2,12,96]{2,1,0:T(8,128)S(1)} %get-tuple-element.620, s32[]{:T(128)S(6)} %copy.213, bf16[12,262144]{1,0:T(8,128)(2,1)} %bitcast.278, pred[96,262144]{1,0:T(32,128)(4,1)} %pad_add_fusion.2), kind=kOutput, calls=%fused_computation.52.clone.1 | convolution fusion | flops 603979776 | bytes 31465476 | tf_op jit(solution)/shard_map/while/body/eval_jaxpr/dot_general | solution.py:49
  761.4 10.0 convolution_convert_fusion.1
  772.8 9.8 convolution_convert_fusion
  790.7 11.0 all-reduce.19
  820.3 7.4 reduce-scatter.21.cloned.1.call-done
  829.6 48.5 %reduce-scatter.15.cloned.1.call-done = bf16[192,3072]{1,0:T(8,128)(2,1)} async-done(((bf16[768,3072]{1,0:T(8,128)(2,1)}), bf16[192,3072]{1,0:T(8,128)(2,1)}) %reduce-scatter.15.cloned.1.call-update) | async-done | bytes 1179664 | tf_op jit(solution)/shard_map/reduce_scatter | solution.py:313
  878.1 50.4 %reduce-scatter.17.cloned.1.call-done = bf16[768,768]{1,0:T(8,128)(2,1)} async-done(((bf16[3072,768]{1,0:T(8,128)(2,1)}), bf16[768,768]{1,0:T(8,128)(2,1)}) %reduce-scatter.17.cloned.1.call-update) | async-done | bytes 1179664 | tf_op jit(solution)/shard_map/reduce_scatter | solution.py:319
  928.5 308.8 %all-reduce.22 = (f32[192,768]{0,1:T(8,128)}, f32[192,768]{0,1:T(8,128)}, f32[192,768]{0,1:T(8,128)}, f32[192,768]{0,1:T(8,128)}, f32[192]{0:T(256)}, /*index=5*...) all-reduce(bf16[192,768]{0,1:T(8,128)(2,1)S(1)} %copy.141, ...), channel_id=1, replica_groups=mesh['dp'=8,'fsdp'=4] {'dp'}, use_global_device_ids=true, to_apply=%region_16.17 | all-reduce | flops 1772064 | bytes 10637568 | tf_op jit(solution)/shard_map/psum | solution.py:332
  (407 shorter events, 176.5 us)
Async XLA Ops:
  7.2 5.5 copy-start.81
  7.2 5.7 copy-start.82
  7.2 5.9 copy-start.83
  7.2 6.2 copy-start.84
  7.3 6.4 copy-start.85
  7.3 6.6 copy-start.86
  7.3 6.8 copy-start.87
  7.3 20.3 %copy-start.77 = (bf16[768]{0:T(1024)(128)(2,1)S(1)}, bf16[768]{0:T(1024)(128)(2,1)}, u32[]{:S(2)}) copy-start(bf16[768]{0:T(1024)(128)(2,1)} %param.38) | copy-start | bytes 4612
  7.3 23.2 %copy-start.78 = (bf16[3,96]{1,0:T(4,128)(2,1)S(1)}, bf16[3,96]{1,0:T(4,128)(2,1)}, u32[]{:S(2)}) copy-start(bf16[3,96]{1,0:T(4,128)(2,1)} %param.34) | copy-start | bytes 1732
  7.3 28.3 %copy-start.67 = (s32[2,1024]{1,0:T(2,128)S(1)}, s32[2,1024]{1,0:T(2,128)}, u32[]{:S(2)}) copy-start(s32[2,1024]{1,0:T(2,128)} %param.25) | copy-start | bytes 24580
  7.3 34.1 %copy-start.21 = (bf16[1024,768]{1,0:T(8,128)(2,1)S(1)}, bf16[1024,768]{1,0:T(8,128)(2,1)}, u32[]{:S(2)}) copy-start(bf16[1024,768]{1,0:T(8,128)(2,1)} %param.43) | copy-start | bytes 4718596
  7.3 37.4 %all-gather.9.cloned.1.call-start = ((), (), s32[]{:S(2)}) async-start(), calls=%async_computation.6 | async-start | bytes 1474560 | tf_op jit(solution)/shard_map/all_gather | solution.py:91
  8.1 44.8 %all-gather.11.cloned.1.call-start = ((), (), s32[]{:S(2)}) async-start(), calls=%async_computation.7 | async-start | bytes 1474560 | tf_op jit(solution)/shard_map/all_gather | solution.py:89
  8.8 34.3 %copy-start.27 = (bf16[1024,768]{1,0:T(8,128)(2,1)S(1)}, bf16[1024,768]{1,0:T(8,128)(2,1)}, u32[]{:S(2)}) copy-start(bf16[1024,768]{1,0:T(8,128)(2,1)} %param.24) | copy-start | bytes 4718596
  8.8 59.4 %all-gather.13.cloned.1.call-start = ((), (), s32[]{:S(2)}) async-start(), calls=%async_computation.8 | async-start | bytes 1474560 | tf_op jit(solution)/shard_map/all_gather | solution.py:90
  9.6 252.8 %all-gather.15.cloned.1.call-start = ((), (), s32[]{:S(2)}) async-start(), calls=%async_computation.9 | async-start | bytes 1474560 | tf_op jit(solution)/shard_map/all_gather | solution.py:92
  10.1 256.6 %all-gather.17.cloned.1.call-start = ((), (), s32[]{:S(2)}) async-start(), calls=%async_computation.10 | async-start | bytes 5898240 | tf_op jit(solution)/shard_map/all_gather | solution.py:99
  10.7 294.3 %all-gather.19.cloned.1.call-start = ((), (), s32[]{:S(2)}) async-start(), calls=%async_computation.11 | async-start | bytes 5898240 | tf_op jit(solution)/shard_map/all_gather | solution.py:101
  11.3 805.5 %reduce-scatter.25.cloned.1.call-start = ((), (), s32[]{:S(2)}) async-start(), calls=%async_computation.17 | async-start | bytes 1474560
  256.5 5.8 copy-start.1
  256.5 5.8 copy-start.3
  256.6 5.8 copy-start.38
  256.6 5.8 copy-start.40
  256.6 5.8 copy-start.42
  256.6 5.8 copy-start.44
  256.6 5.8 copy-start.46
  256.6 5.8 copy-start.73
  266.2 38.7 %copy-start.18 = (f32[1024,768]{0,1:T(8,128)}, f32[1024,768]{0,1:T(8,128)S(1)}, u32[]{:S(2)}) copy-start(f32[1024,768]{0,1:T(8,128)S(1)} %get-tuple-element.390) | copy-start | bytes 9437188
  266.3 83.1 %copy-start.56 = (f32[1024]{0:T(1024)}, f32[1024]{0:T(1024)S(1)}, u32[]{:S(2)}) copy-start(f32[1024]{0:T(1024)S(1)} %broadcast_multiply_fusion.8) | copy-start | bytes 12292
  266.7 82.7 %copy-start.60 = (f32[1024]{0:T(1024)}, f32[1024]{0:T(1024)S(1)}, u32[]{:S(2)}) copy-start(f32[1024]{0:T(1024)S(1)} %fusion.70) | copy-start | bytes 12292
  267.0 38.0 %copy-start.72 = (f32[768]{0:T(1024)S(1)}, f32[768]{0:T(1024)}, u32[]{:S(2)}) copy-start(f32[768]{0:T(1024)} %convert_element_type.211) | copy-start | bytes 9220
  305.0 9.7 copy-start.11
  305.0 9.7 copy-start.48
  314.7 22.9 %copy-start.7 = (f32[1024,768]{0,1:T(8,128)}, f32[1024,768]{0,1:T(8,128)S(1)}, u32[]{:S(2)}) copy-start(f32[1024,768]{0,1:T(8,128)S(1)} %get-tuple-element.393) | copy-start | bytes 9437188
  314.7 22.9 %copy-start.50 = (f32[1024]{0:T(1024)}, f32[1024]{0:T(1024)S(1)}, u32[]{:S(2)}) copy-start(f32[1024]{0:T(1024)S(1)} %broadcast_multiply_fusion.7) | copy-start | bytes 12292
  315.5 22.1 %copy-start.52 = (f32[1024]{0:T(1024)}, f32[1024]{0:T(1024)S(1)}, u32[]{:S(2)}) copy-start(f32[1024]{0:T(1024)S(1)} %get-tuple-element.386) | copy-start | bytes 12292
  319.6 18.0 %copy-start.35 = (bf16[1024,768]{0,1:T(8,128)(2,1)}, bf16[1024,768]{0,1:T(8,128)(2,1)S(1)}, u32[]{:S(2)}) copy-start(bf16[1024,768]{0,1:T(8,128)(2,1)S(1)} %get-tuple-element.370) | copy-start | bytes 4718596
  337.6 11.8 copy-start.19
  355.3 462.6 %reduce-scatter.23.cloned.1.call-start = ((), (), s32[]{:S(2)}) async-start(), calls=%async_computation.16 | async-start | bytes 1474560
  384.1 31.9 %copy-start.5 = (bf16[2,512,12,64]{1,3,2,0:T(8,128)(2,1)}, bf16[2,512,12,64]{1,3,2,0:T(8,128)(2,1)S(1)}, u32[]{:S(2)}) copy-start(bf16[2,512,12,64]{1,3,2,0:T(8,128)(2,1)S(1)} %get-tuple-element.644) | copy-start | bytes 4718596 | tf_op jit(solution)/shard_map/while
  495.7 6.9 copy-start.13
  502.6 6.4 copy-start
  511.3 9.2 copy-start.16
  538.6 17.0 %copy-start.6 = (bf16[2,512,12,64]{1,3,2,0:T(8,128)(2,1)S(1)}, bf16[2,512,12,64]{1,3,2,0:T(8,128)(2,1)}, u32[]{:S(2)}) copy-start(bf16[2,512,12,64]{1,3,2,0:T(8,128)(2,1)} %copy-done.5) | copy-start | bytes 4718596 | tf_op jit(solution)/shard_map/while
  555.7 31.9 %copy-start.5 = (bf16[2,512,12,64]{1,3,2,0:T(8,128)(2,1)}, bf16[2,512,12,64]{1,3,2,0:T(8,128)(2,1)S(1)}, u32[]{:S(2)}) copy-start(bf16[2,512,12,64]{1,3,2,0:T(8,128)(2,1)S(1)} %get-tuple-element.644) | copy-start | bytes 4718596 | tf_op jit(solution)/shard_map/while
  667.3 6.9 copy-start.13
  674.2 6.4 copy-start
  682.9 9.2 copy-start.16
  710.3 17.0 %copy-start.6 = (bf16[2,512,12,64]{1,3,2,0:T(8,128)(2,1)S(1)}, bf16[2,512,12,64]{1,3,2,0:T(8,128)(2,1)}, u32[]{:S(2)}) copy-start(bf16[2,512,12,64]{1,3,2,0:T(8,128)(2,1)} %copy-done.5) | copy-start | bytes 4718596 | tf_op jit(solution)/shard_map/while
  735.1 4.8 copy-start.29
  744.8 74.4 %reduce-scatter.19.cloned.1.call-start = ((), (), s32[]{:S(2)}) async-start(), calls=%async_computation.14 | async-start | bytes 1474560
  753.1 74.6 %reduce-scatter.21.cloned.1.call-start = ((), (), s32[]{:S(2)}) async-start(), calls=%async_computation.15 | async-start | bytes 1474560
  761.3 116.8 %reduce-scatter.15.cloned.1.call-start = ((), (), s32[]{:S(2)}) async-start(), calls=%async_computation.12 | async-start | bytes 5898240 | tf_op jit(solution)/shard_map/reduce_scatter | solution.py:313
  771.5 157.1 %reduce-scatter.17.cloned.1.call-start = ((), (), s32[]{:S(2)}) async-start(), calls=%async_computation.13 | async-start | bytes 5898240 | tf_op jit(solution)/shard_map/reduce_scatter | solution.py:319
  782.6 8.0 copy-start.64
  782.7 8.0 copy-start.65
  782.7 8.0 copy-start.66
  782.7 8.0 copy-start.68
  782.7 8.0 copy-start.74
  782.7 8.0 copy-start.75
  782.7 19.0 %copy-start.8 = (f32[1024,768]{0,1:T(8,128)S(1)}, f32[1024,768]{0,1:T(8,128)}, u32[]{:S(2)}) copy-start(f32[1024,768]{0,1:T(8,128)} %copy-done.7) | copy-start | bytes 9437188
  782.7 19.0 %copy-start.49 = (f32[768]{0:T(1024)S(1)}, f32[768]{0:T(1024)}, u32[]{:S(2)}) copy-start(f32[768]{0:T(1024)} %convert_element_type.212) | copy-start | bytes 9220
  782.7 19.0 %copy-start.51 = (f32[1024]{0:T(1024)S(1)}, f32[1024]{0:T(1024)}, u32[]{:S(2)}) copy-start(f32[1024]{0:T(1024)} %copy-done.50) | copy-start | bytes 12292
  782.7 19.0 %copy-start.53 = (f32[1024]{0:T(1024)S(1)}, f32[1024]{0:T(1024)}, u32[]{:S(2)}) copy-start(f32[1024]{0:T(1024)} %copy-done.52) | copy-start | bytes 12292
  (49 other events, 129.7 us)
Sparse Core Ops, SparseCore 0:
  9.7 20.3 all-gather.8
  31.6 17.4 all-gather.10
  50.7 17.4 all-gather.12
  69.6 17.4 all-gather.14
  88.5 37.4 all-gather.16
  127.4 37.4 all-gather.18
  355.4 25.7 reduce-scatter.24
  744.9 25.7 reduce-scatter.22
  773.2 26.0 reduce-scatter.18
  802.0 25.6 reduce-scatter.20
  830.2 47.8 reduce-scatter.14
  880.7 47.8 reduce-scatter.16
where the time goes:
time: 1280 us; the launch traced here: 1270 us
  blocking collectives  343 us (27%)
  matrix products  304 us (24%)
  local copies, waits for them, and re-layouts  300 us (23%)
  other arithmetic  155 us (12%)
  waiting for transfers between devices  120 us (9%)
  loops' own time  28.6 us (2%)
  between operations  18.6 us (1%)
    psum x1, blocking collectives, on_device(): lax.psum((parts[0], parts[1], parts[2], parts[3], parts[4], parts[5], par...  309 us
    while x68, local copies, waits for them, and re-layouts  116 us
    reshape x8, local copies, waits for them, and re-layouts, window_scores(): jnp.dot(table, onehot, preferred_element_type=jnp.float32)  94.8 us
    dot_general x4, matrix products, window_scores(): jnp.dot(table, onehot, preferred_element_type=jnp.float32)  71.3 us
    dot_general x8, matrix products, times_transposed(): lax.dot_general(left, weight, (((1,), (1,)), ((), ())), preferred_element...  70.8 us
    eq x12, other arithmetic, bucket_onehot(): tables.append(relative.reshape(1, -1) == labels[:, None])  64.5 us
    reduce_scatter x1, waiting for transfers between devices, on_device(): lax.psum_scatter(grad_down.astype(jnp.bfloat16), 'fsdp', scatter_dimensio...  50.4 us
    reduce_scatter x1, waiting for transfers between devices, on_device(): lax.psum_scatter(grad_up.astype(jnp.bfloat16), 'fsdp', scatter_dimension=...  48.5 us
  transfers between devices with their start and end apart: 12, of which 4 were waited for; matrix products, arithmetic and copies ran while one was open for 53% of the time, Pallas kernels for 0%

commit v1 on v0

v1 whole, which is shorter than its diff:
```python
import functools
import math

import jax
import jax.numpy as jnp
import numpy as np
from jax import lax
from jax.experimental import pallas as pl
from jax.experimental.pallas import tpu as pltpu
from jax.sharding import PartitionSpec as P

HEADS = 12
HD = 64
WIN = 512
BUCKETS = 32
PAIRS = HEADS // 2
SCALE = HD ** (-0.5)
EPS = 1e-05
BF = jnp.bfloat16
F32 = jnp.float32
VMEM_LIMIT = 60 * 1024 * 1024
GROUPS = ((0, 2), (2, 2), (4, 2))


def params():
    return pltpu.CompilerParams(vmem_limit_bytes=VMEM_LIMIT)


def cost(flops, nbytes, transcendentals=0):
    return pl.CostEstimate(
        flops=int(flops), bytes_accessed=int(nbytes), transcendentals=int(transcendentals)
    )


def struct(shape, dtype):
    return jax.ShapeDtypeStruct(shape, dtype)


def dot(left, right):
    return lax.dot_general(left, right, (((1,), (0,)), ((), ())), preferred_element_type=F32)


def dot_t(left, right):
    return lax.dot_general(left, right, (((1,), (1,)), ((), ())), preferred_element_type=F32)


def tdot(left, right):
    return lax.dot_general(left, right, (((0,), (0,)), ((), ())), preferred_element_type=F32)


def split3(values):
    high = values.astype(BF)
    rest = values - high.astype(F32)
    middle = rest.astype(BF)
    return high, middle, (rest - middle.astype(F32)).astype(BF)


def swap(array, axis, bit):
    return lax.ppermute(array, axis, [(i, i ^ bit) for i in range(lax.axis_size(axis))])


def half_of(array, which, axis=0):
    rows = array.shape[axis] // 2
    return lax.dynamic_slice_in_dim(array, which * rows, rows, axis)


def gather(shard, parity):
    far = swap(half_of(shard, parity), "fsdp", 2)
    beside = swap(far, "dp", 1)
    return (
        shard,
        swap(shard, "fsdp", 1),
        far,
        beside,
        swap(far, "fsdp", 1),
        swap(beside, "fsdp", 1),
    )


def part_rows(index, rows):
    me, parity = index[0], index[1]
    half = rows // 2
    return (
        (me * rows, rows),
        ((me ^ 1) * rows, rows),
        ((me ^ 2) * rows + parity * half, half),
        ((me ^ 2) * rows + (1 - parity) * half, half),
        ((me ^ 3) * rows + parity * half, half),
        ((me ^ 3) * rows + (1 - parity) * half, half),
    )


PARTS = 6


def fetch_copies(index, parts, whole, sems):
    rows = whole.shape[0] // 4
    return [
        pltpu.make_async_copy(part, whole.at[pl.ds(pl.multiple_of(first, 16), count)], sems.at[at])
        for at, (part, (first, count)) in enumerate(zip(parts, part_rows(index, rows)))
    ]


ANY = pl.BlockSpec(memory_space=pl.ANY)
SMEM = pl.BlockSpec(memory_space=pltpu.SMEM)


def reduce_rows(keep, send, factor):
    place = lax.axis_index("dp")
    near, beside = place & 1, (place >> 1) & 1
    got = swap(send, "fsdp", 1)
    far = swap((keep[1].astype(F32) + got[1].astype(F32)).astype(BF), "fsdp", 2)

    def part(which, arrays):
        return sum(half_of(a, which).astype(F32) for a in arrays).astype(BF)

    terms = (keep[0], got[0], far)
    terms = (part(near, terms), swap(part(1 - near, terms), "dp", 1))
    other = swap(part(1 - beside, terms), "dp", 2)
    total = (part(beside, terms).astype(F32) + other.astype(F32)).astype(BF)
    bit = 4
    while bit < lax.axis_size("dp"):
        total = (total.astype(F32) + swap(total, "dp", bit).astype(F32)).astype(BF)
        bit *= 2
    other = swap(total, "dp", 2)
    total = in_order(total, other, beside)
    other = swap(total, "dp", 1)
    return in_order(total, other, near).astype(F32) * factor


def in_order(mine, other, which):
    return jnp.where(
        which == 0, jnp.concatenate([mine, other]), jnp.concatenate([other, mine])
    )


def table_places():
    span = np.arange(128)
    step = np.where(span < 64, span, span - 128)
    near = np.clip(step, -16, 15) + 16
    far = np.where(step <= -2, 0, np.where(step >= 2, 31, -1))
    wide = np.arange(256)
    wide = np.where(wide < 128, wide, wide - 256)
    return np.concatenate(
        [
            near + 32,
            near + 64,
            far,
            np.clip(wide, -16, 15) + 16,
            np.clip(-wide, -16, 15) + 16,
        ]
    ).astype(np.int32)


LANES = 896


def iota(shape, axis):
    return lax.broadcasted_iota(jnp.int32, shape, axis)


def as_bf(mask):
    return jnp.where(mask, 1.0, 0.0).astype(BF)


def near_tile(row):
    rolled = pltpu.roll(jnp.broadcast_to(row, (128, 256)), 0, 1, stride=1, stride_axis=0)
    r, c = iota((128, 256), 0), iota((128, 256), 1)
    gap = (r >> 4) - (c >> 4)
    inside = (c < 128) & (gap <= 1) & (gap >= -1)
    corner = ((r >= 112) & (c >= 128) & (c < 144)) | ((r < 16) & (c >= 240))
    return jnp.where(inside | corner, rolled, 0.0)


def prep_kernel(cols_ref, rows_ref, lanes_ref, e_ref, ke_ref, ket_ref, oh_ref, d_ref, dt_ref, own):
    tokens = cols_ref.shape[0]

    @pl.when(pl.program_id(0) == 0)
    def _():
        x, y, valid = cols_ref[:, 0:1], cols_ref[:, 1:2], cols_ref[:, 2:3]
        lane = iota((tokens, 128), 1)
        block = (iota((tokens, 128), 0) & (WIN - 1)) >> 4
        third = lane >> 5
        hot = jnp.where(third == 0, x, jnp.where(third == 1, y + 32, block + 64)) == lane
        hot = hot & (lane < 96)
        own[...] = as_bf(hot | (lane == 96))
        back = jnp.where(third == 0, 31 - x, jnp.where(third == 1, 63 - y, 95 - block)) == lane
        oh_ref[...] = as_bf(back & (lane < 96))
        masked = jnp.where((lane == 99) & (valid <= 0), -1e30, 0.0)
        ones = hot | ((lane >= 96) & (lane < 99))
        ke_ref[...] = jnp.where(ones, 1.0, masked).astype(BF)
        x, y, valid = rows_ref[0:1, :], rows_ref[1:2, :], rows_ref[2:3, :]
        lane = iota((128, tokens), 0)
        block = (iota((128, tokens), 1) & (WIN - 1)) >> 4
        third = lane >> 5
        hot = jnp.where(third == 0, x, jnp.where(third == 1, y + 32, block + 64)) == lane
        hot = hot & (lane < 96)
        masked = jnp.where((lane == 99) & (valid <= 0), -1e30, 0.0)
        ones = hot | ((lane >= 96) & (lane < 99))
        ket_ref[...] = jnp.where(ones, 1.0, masked).astype(BF)

    row = lanes_ref[0]
    lane = iota((32, 128), 1)
    blocks = []
    for at in range(3):
        spread = jnp.broadcast_to(row[:, at * 128 : at * 128 + 128], (32, 128))
        spread = pltpu.roll(spread, at * 32, 1, stride=1, stride_axis=0)
        blocks.append(jnp.where(lane >> 5 == at, spread, 0.0))
    blocks.append(jnp.where((iota((32, 128), 0) == 0) & (lane == 99), 1.0, 0.0))
    e_ref[...] = dot(own[...], jnp.concatenate(blocks, axis=0).astype(BF)).astype(BF)
    d_ref[0] = near_tile(row[:, 384:640])
    dt_ref[0] = near_tile(row[:, 640:896])


def prepare(layout_cells, pad_mask, table):
    tokens = pad_mask.shape[0]
    rows = jnp.concatenate([layout_cells, pad_mask[None], jnp.zeros_like(layout_cells)[:1]])
    places = jnp.asarray(table_places())
    pick = (jnp.arange(96, dtype=jnp.int32)[:, None] == places[None, :]).astype(BF)
    lanes = jnp.dot(table, pick, preferred_element_type=F32).reshape(HEADS, 1, LANES)
    whole = lambda h: (0, 0)
    return pl.pallas_call(
        prep_kernel,
        grid=(HEADS,),
        in_specs=[
            pl.BlockSpec((tokens, 4), whole),
            pl.BlockSpec((4, tokens), whole),
            pl.BlockSpec((1, 1, LANES), lambda h: (h, 0, 0)),
        ],
        out_specs=[
            pl.BlockSpec((tokens, 128), lambda h: (0, h)),
            pl.BlockSpec((tokens, 128), whole),
            pl.BlockSpec((128, tokens), whole),
            pl.BlockSpec((tokens, 128), whole),
            pl.BlockSpec((1, 128, 256), lambda h: (h, 0, 0)),
            pl.BlockSpec((1, 128, 256), lambda h: (h, 0, 0)),
        ],
        out_shape=[
            struct((tokens, HEADS * 128), BF),
            struct((tokens, 128), BF),
            struct((128, tokens), BF),
            struct((tokens, 128), BF),
            struct((HEADS, 128, 256), F32),
            struct((HEADS, 128, 256), F32),
        ],
        scratch_shapes=[pltpu.VMEM((tokens, 128), BF)],
        compiler_params=params(),
        cost_estimate=cost(2 * tokens * 128 * 128 * HEADS, 7e6),
        name="prepare",
    )(rows.T, rows, lanes)


def project_kernel(index, *refs):
    parts, (x_ref, bias_ref, out_ref, weight, sems) = refs[:PARTS], refs[PARTS:]

    @pl.when(pl.program_id(0) == 0)
    def _():
        copies = fetch_copies(index, parts, weight, sems)
        for copy in copies:
            copy.start()
        for copy in copies:
            copy.wait()

    width = out_ref.shape[1] // 3
    for at in range(3):
        span = slice(at * width, (at + 1) * width)
        values = dot(x_ref[...], weight[:, span])
        if at == 0:
            values = (values + bias_ref[0:1, :]).astype(BF) * SCALE
        if at == 2:
            values = values + bias_ref[1:2, :]
        out_ref[:, span] = values.astype(BF)


def project(index, parts, tokens, biases, block=256):
    rows, width = tokens.shape
    return pl.pallas_call(
        project_kernel,
        grid=(rows // block,),
        in_specs=[SMEM]
        + [ANY] * PARTS
        + [
            pl.BlockSpec((block, width), lambda i: (i, 0)),
            pl.BlockSpec((2, width), lambda i: (0, 0)),
        ],
        out_specs=pl.BlockSpec((block, 3 * width), lambda i: (i, 0)),
        out_shape=struct((rows, 3 * width), BF),
        scratch_shapes=[pltpu.VMEM((width, 3 * width), BF), pltpu.SemaphoreType.DMA((PARTS,))],
        compiler_params=params(),
        cost_estimate=cost(6 * rows * width * width, 10e6),
        name="project",
    )(index, *parts, tokens, biases)


def input_kernel(index, *refs):
    count = len(GROUPS) * 3
    parts, grads = refs[:PARTS], refs[PARTS : PARTS + count]
    dresid_ref, out_ref, weight, sems = refs[PARTS + count :]

    @pl.when(pl.program_id(0) == 0)
    def _():
        copies = fetch_copies(index, parts, weight, sems)
        for copy in copies:
            copy.start()
        for copy in copies:
            copy.wait()

    joined = jnp.concatenate(
        [grads[3 * group + at][...] for at in range(3) for group in range(len(GROUPS))], axis=1
    )
    out_ref[...] = (dresid_ref[...] + dot_t(joined, weight[...])).astype(BF)


def input_gradient(index, parts, grads, dresid, block=256):
    rows, width = dresid.shape
    spec = lambda a: pl.BlockSpec((block, a.shape[1]), lambda i: (i, 0))
    return pl.pallas_call(
        input_kernel,
        grid=(rows // block,),
        in_specs=[SMEM] + [ANY] * PARTS + [spec(a) for a in grads] + [spec(dresid)],
        out_specs=spec(dresid),
        out_shape=struct((rows, width), BF),
        scratch_shapes=[pltpu.VMEM((width, 3 * width), BF), pltpu.SemaphoreType.DMA((PARTS,))],
        compiler_params=params(),
        cost_estimate=cost(6 * rows * width * width, 13e6),
        name="input_gradient",
    )(index, *parts, *grads, dresid)


def with_near(pieces, tile, at):
    pieces = list(pieces)
    pieces[at] = pieces[at] + tile[:, :128]
    if at > 0:
        left = pieces[at - 1]
        pieces[at - 1] = jnp.concatenate([left[:16] + tile[:16, 128:], left[16:]], axis=0)
    if at < 3:
        right = pieces[at + 1]
        pieces[at + 1] = jnp.concatenate([right[:112], right[112:] + tile[112:, 128:]], axis=0)
    return pieces


def lane_blocks(values):
    return [values[:, c * 128 : c * 128 + 128] for c in range(WIN // 128)]


def attend_kernel(q_ref, k_ref, v_ref, e_ref, ket_ref, d_ref, out_ref, eout_ref):
    first = iota((WIN, 128), 1) < HD
    keys = jnp.concatenate([k_ref[...].T, ket_ref[...]], axis=0)
    mixed = []
    for head in range(2):
        mine = first if head == 0 else ~first
        span = slice(head * 128, head * 128 + 128)
        extra = e_ref[:, span]
        query = jnp.concatenate([jnp.where(mine, q_ref[...], jnp.zeros((), BF)), extra], axis=1)
        tile = d_ref[head]
        rows, logs = [], []
        for at in range(WIN // 128):
            scores = dot(query[at * 128 : at * 128 + 128], keys)
            pieces = with_near(lane_blocks(scores), tile, at)
            top = jnp.maximum(
                jnp.maximum(pieces[0], pieces[1]), jnp.maximum(pieces[2], pieces[3])
            )
            top = jnp.max(top, axis=1, keepdims=True)
            pieces = [jnp.exp(piece - top) for piece in pieces]
            total = jnp.sum(
                (pieces[0] + pieces[1]) + (pieces[2] + pieces[3]), axis=1, keepdims=True
            )
            weights = jnp.concatenate([piece.astype(BF) for piece in pieces], axis=1)
            rows.append(dot(weights, v_ref[...]) / total)
            logs.append(top + jnp.log(total))
        mixed.append(jnp.concatenate(rows, axis=0))
        lane = iota((WIN, 128), 1)
        parts = split3(-jnp.concatenate(logs, axis=0))
        for at in range(3):
            extra = jnp.where(lane == 96 + at, parts[at], extra)
        eout_ref[:, span] = extra
    out_ref[...] = jnp.where(first, mixed[0], mixed[1]).astype(BF)


def attend(qkv, extra, ket, near):
    tokens = qkv.shape[0]
    windows = tokens // WIN
    head_block = lambda shift: pl.BlockSpec((WIN, 128), lambda p, w: (w, p + shift))
    wide = pl.BlockSpec((WIN, 256), lambda p, w: (w, p))
    return pl.pallas_call(
        attend_kernel,
        grid=(PAIRS, windows),
        in_specs=[
            head_block(0),
            head_block(PAIRS),
            head_block(2 * PAIRS),
            wide,
            pl.BlockSpec((128, WIN), lambda p, w: (0, w)),
            pl.BlockSpec((2, 128, 256), lambda p, w: (p, 0, 0)),
        ],
        out_specs=[pl.BlockSpec((WIN, 128), lambda p, w: (w, p)), wide],
        out_shape=[struct((tokens, PAIRS * 128), BF), struct((tokens, HEADS * 128), BF)],
        compiler_params=params(),
        cost_estimate=cost(tokens * WIN * HEADS * 768, 17e6, tokens * WIN * HEADS),
        name="attend",
    )(qkv, qkv, qkv, extra, ket, near)


def diagonal_rows(sums):
    lane = iota((32, 128), 1)
    rows = []
    for at in range(3):
        block = jnp.where(lane >> 5 == at, sums[at * 32 : at * 32 + 32], 0.0)
        rolled = pltpu.roll(block, 0, 1, stride=1, stride_axis=0)
        rows.append(jnp.sum(rolled, axis=0, keepdims=True))
    return rows


def near_rows(tile):
    r, c = iota((128, 256), 0), iota((128, 256), 1)
    gap = (r >> 4) - (c >> 4)
    inside = (c < 128) & (gap <= 1) & (gap >= -1)
    corner = ((r >= 112) & (c >= 128) & (c < 144)) | ((r < 16) & (c >= 240))
    tile = jnp.where(inside | corner, tile, 0.0)
    turn = as_bf(iota((128, 128), 0) + iota((128, 128), 1) == 127)
    high, middle, low = split3(tile)
    turned = dot(turn, high) + dot(turn, middle) + dot(turn, low)
    rolled = pltpu.roll(turned, 0, 1, stride=1, stride_axis=0)
    return jnp.sum(rolled, axis=0, keepdims=True)


def attend_back_kernel(
    q_ref, k_ref, v_ref, e_ref, ke_ref, ket_ref, oh_ref, dt_ref, do_ref, o_ref,
    dq_ref, dk_ref, dv_ref, far_ref, near_ref,
    p_scr, ds_scr, sums, tiles,
):
    window = pl.program_id(1)
    zero = jnp.zeros((), BF)
    first = iota((WIN, 128), 1) < HD
    lane = iota((WIN, 128), 1)
    keys = jnp.concatenate([k_ref[...], ke_ref[...]], axis=1)
    values = jnp.concatenate([v_ref[...], ke_ref[...]], axis=1)
    keys_t = k_ref[...].T
    product = do_ref[...].astype(F32) * o_ref[...].astype(F32)
    dq_t, dk, dv = [], None, None
    for head in range(2):
        mine = first if head == 0 else ~first
        query = jnp.where(mine, q_ref[...], zero)
        grad = jnp.where(mine, do_ref[...], zero)
        delta = -jnp.sum(jnp.where(mine, product, 0.0), axis=1, keepdims=True)
        parts = split3(delta)
        minus = jnp.zeros((WIN, 128), BF)
        for at in range(3):
            minus = jnp.where(lane == 96 + at, parts[at], minus)
        query_all = jnp.concatenate([query, e_ref[:, head * 128 : head * 128 + 128]], axis=1)
        grad_all = jnp.concatenate([grad, minus], axis=1)
        tile = dt_ref[head]
        diag, low, high = None, None, None
        for at in range(WIN // 128):
            rows = slice(at * 128, at * 128 + 128)
            scores = with_near(lane_blocks(dot_t(keys[rows], query_all)), tile, at)
            probs = [jnp.exp(piece) for piece in scores]
            dprobs = lane_blocks(dot_t(values[rows], grad_all))
            dscores = [a * b for a, b in zip(probs, dprobs)]
            p_scr[rows] = jnp.concatenate([a.astype(BF) for a in probs], axis=1)
            ds_scr[rows] = jnp.concatenate([a.astype(BF) for a in dscores], axis=1)
            add = lambda total, term: term if total is None else total + term
            diag = add(diag, dscores[at])
            if at > 0:
                low = add(low, dscores[at - 1][:16])
            if at < 3:
                high = add(high, dscores[at + 1][112:])
        dscores = ds_scr[...]
        dv_head = dot(p_scr[...], grad)
        dk_head = dot(dscores, query)
        dv = dv_head if dv is None else dv + dv_head
        dk = dk_head if dk is None else dk + dk_head
        left = jnp.concatenate([keys_t[head * HD : head * HD + HD], ket_ref[:96]], axis=0)
        both = dot(left, dscores)
        dq_t.append(both[:HD] * SCALE)
        extra = both[HD:]
        extra_high = extra.astype(BF)
        extra_low = (extra - extra_high.astype(F32)).astype(BF)
        far = dot(extra_high, oh_ref[...]) + dot(extra_low, oh_ref[...])

        @pl.when(window == 0)
        def _():
            sums[head] = far
            tiles[head] = jnp.zeros((128, 256), F32)

        @pl.when(window > 0)
        def _():
            sums[head] = sums[head] + far

        tiles[head, :, :128] = tiles[head, :, :128] + diag
        tiles[head, :16, 128:] = tiles[head, :16, 128:] + low
        tiles[head, 112:, 128:] = tiles[head, 112:, 128:] + high
    dq_ref[...] = jnp.concatenate(dq_t, axis=0).T.astype(BF)
    dk_ref[...] = dk.astype(BF)
    dv_ref[...] = dv.astype(BF)

    @pl.when(window == pl.num_programs(1) - 1)
    def _():
        for head in range(2):
            rows = diagonal_rows(sums[head])
            far_ref[head] = jnp.concatenate(rows + [jnp.zeros((5, 128), F32)], axis=0)
            near_ref[head] = jnp.broadcast_to(near_rows(tiles[head]), (8, 256))


def attend_back(group, qkv, extra, ke, ket, oh, near_t, dmixed, mixed):
    start, pairs = group
    tokens = qkv.shape[0]
    windows = tokens // WIN
    block = lambda shift: pl.BlockSpec((WIN, 128), lambda p, w: (w, p + start + shift))
    per_window = pl.BlockSpec((WIN, 128), lambda p, w: (w, 0))
    out = pl.BlockSpec((WIN, 128), lambda p, w: (w, p))
    out_rows = struct((tokens, pairs * 128), BF)
    return pl.pallas_call(
        attend_back_kernel,
        grid=(pairs, windows),
        in_specs=[
            block(0),
            block(PAIRS),
            block(2 * PAIRS),
            pl.BlockSpec((WIN, 256), lambda p, w: (w, p + start)),
            per_window,
            pl.BlockSpec((128, WIN), lambda p, w: (0, w)),
            per_window,
            pl.BlockSpec((2, 128, 256), lambda p, w: (p + start, 0, 0)),
            block(0),
            block(0),
        ],
        out_specs=[
            out,
            out,
            out,
            pl.BlockSpec((2, 8, 128), lambda p, w: (p, 0, 0)),
            pl.BlockSpec((2, 8, 256), lambda p, w: (p, 0, 0)),
        ],
        out_shape=[
            out_rows,
            out_rows,
            out_rows,
            struct((2 * pairs, 8, 128), F32),
            struct((2 * pairs, 8, 256), F32),
        ],
        scratch_shapes=[
            pltpu.VMEM((WIN, WIN), BF),
            pltpu.VMEM((WIN, WIN), BF),
            pltpu.VMEM((2, 96, 128), F32),
            pltpu.VMEM((2, 128, 256), F32),
        ],
        compiler_params=params(),
        cost_estimate=cost(
            tokens * WIN * pairs * 2 * 2048, 12e6, tokens * WIN * pairs * 2
        ),
        name="attend_back",
    )(qkv, qkv, qkv, extra, ke, ket, oh, near_t, dmixed, mixed)


def table_gradient(far, near):
    lane = np.arange(128)
    entry = np.clip(lane - 31, -16, 15) + 16
    x_place = np.where(lane < 63, entry + 32, -1)
    y_place = np.where((lane >= 32) & (lane < 95), np.clip(lane - 63, -16, 15) + 16 + 64, -1)
    block_step = lane - 95
    blk_place = np.where(
        (lane >= 64) & (block_step <= -2), 0, np.where((lane < 127) & (block_step >= 2), 31, -1)
    )
    wide = np.arange(256)
    step = (127 - wide + 128) % 256 - 128
    near_place = np.clip(step, -16, 15) + 16
    places = np.concatenate([x_place, y_place, blk_place, near_place]).astype(np.int32)
    sums = jnp.concatenate([far[:, 0], far[:, 1], far[:, 2], near[:, 0]], axis=1)
    pick = (jnp.asarray(places)[:, None] == jnp.arange(96, dtype=jnp.int32)[None, :]).astype(F32)
    return jnp.dot(sums, pick, precision=lax.Precision.HIGHEST, preferred_element_type=F32)


def norm_parts(values):
    centre = values - jnp.mean(values, axis=-1, keepdims=True)
    spread = jnp.mean(centre * centre, axis=-1, keepdims=True)
    scale = lax.rsqrt(spread + EPS)
    return centre * scale, scale


def norm_back(grad, hat, scale):
    mean = jnp.mean(grad, axis=-1, keepdims=True)
    along = jnp.mean(grad * hat, axis=-1, keepdims=True)
    return scale * (grad - mean - hat * along)


def add_rows(ref, rows):
    for at, values in enumerate(rows):
        ref[at : at + 1, :] += jnp.sum(values.astype(F32), axis=0, keepdims=True)


def start_copies(copies):
    for copy in copies:
        copy.start()


def wait_copies(copies):
    for copy in copies:
        copy.wait()


def forward_kernel(index, *refs):
    parts = [refs[at * PARTS : at * PARTS + PARTS] for at in range(3)]
    (
        mixed_ref, x_ref, cot_ref, small_ref, up_bias_ref,
        out_ref, dfinal_ref, dbranch_ref, active_ref, slope_ref, normed_ref, resid_ref, sums_ref,
        w_out, w_up, w_down, sems,
    ) = refs[3 * PARTS :]
    step = pl.program_id(0)
    weights = (w_out, w_up, w_down)
    copies = [fetch_copies(index, parts[at], weights[at], sems.at[at]) for at in range(3)]

    @pl.when(step == 0)
    def _():
        sums_ref[...] = jnp.zeros_like(sums_ref)
        for group in copies:
            start_copies(group)
        wait_copies(copies[0])

    small = lambda at: small_ref[at : at + 1, :]
    attended = dot(mixed_ref[...], w_out[...]) + small(0)
    resid = x_ref[...].astype(F32) + attended
    resid_ref[...] = resid
    hat, _ = norm_parts(resid)
    normed = hat * small(1) + small(2)
    low = normed.astype(BF)
    normed_ref[...] = low

    @pl.when(step == 0)
    def _():
        wait_copies(copies[1])
        wait_copies(copies[2])

    width = w_down.shape[1]
    branch = None
    for at in range(w_up.shape[1] // width):
        span = slice(at * width, at * width + width)
        hidden = dot(low, w_up[:, span]) + up_bias_ref[:, span]
        upto = 0.5 + 0.5 * lax.erf(hidden * math.sqrt(0.5))
        density = jnp.exp(hidden * hidden * -0.5) * (1.0 / math.sqrt(2.0 * math.pi))
        slope_ref[:, span] = (upto + hidden * density).astype(BF)
        active = (hidden * upto).astype(BF)
        active_ref[:, span] = active
        term = dot(active, w_down[span, :])
        branch = term if branch is None else branch + term
    final = normed + branch + small(3)
    hat, scale = norm_parts(final)
    out_ref[...] = (hat * small(4) + small(5)).astype(BF)
    cot = cot_ref[...].astype(F32)
    dfinal = norm_back(cot * small(4), hat, scale)
    dfinal_ref[...] = dfinal
    dbranch = dfinal.astype(BF)
    dbranch_ref[...] = dbranch
    add_rows(sums_ref, (cot * hat, cot, dbranch))


def forward(index, parts, mixed, tokens, cotangent, smalls, up_bias, block=256):
    rows, width = tokens.shape
    hidden = up_bias.shape[1]
    narrow = pl.BlockSpec((block, width), lambda i: (i, 0))
    wide = pl.BlockSpec((block, hidden), lambda i: (i, 0))
    whole = lambda a: pl.BlockSpec(a.shape, lambda i: (0, 0))
    return pl.pallas_call(
        forward_kernel,
        grid=(rows // block,),
        in_specs=[SMEM]
        + [ANY] * (3 * PARTS)
        + [narrow, narrow, narrow, whole(smalls), whole(up_bias)],
        out_specs=[
            narrow, narrow, narrow, wide, wide, narrow, narrow,
            pl.BlockSpec((8, width), lambda i: (0, 0)),
        ],
        out_shape=[
            struct((rows, width), BF),
            struct((rows, width), F32),
            struct((rows, width), BF),
            struct((rows, hidden), BF),
            struct((rows, hidden), BF),
            struct((rows, width), BF),
            struct((rows, width), F32),
            struct((8, width), F32),
        ],
        scratch_shapes=[
            pltpu.VMEM((width, width), BF),
            pltpu.VMEM((width, hidden), BF),
            pltpu.VMEM((hidden, width), BF),
            pltpu.SemaphoreType.DMA((3, PARTS)),
        ],
        compiler_params=params(),
        cost_estimate=cost(2 * rows * width * (width + 2 * hidden), 40e6, 3 * rows * hidden),
        name="forward",
    )(index, *parts[0], *parts[1], *parts[2], mixed, tokens, cotangent, smalls, up_bias)


def backward_kernel(index, *refs):
    parts = [refs[at * PARTS : at * PARTS + PARTS] for at in range(3)]
    (
        dbranch_ref, slope_ref, dfinal_ref, resid_ref, small_ref,
        dhidden_ref, dresid_ref, dattn_ref, dmixed_ref, sums_ref, up_sums_ref,
        w_out, w_up, w_down, sems,
    ) = refs[3 * PARTS :]
    step = pl.program_id(0)
    weights = (w_out, w_up, w_down)
    copies = [fetch_copies(index, parts[at], weights[at], sems.at[at]) for at in range(3)]

    @pl.when(step == 0)
    def _():
        sums_ref[...] = jnp.zeros_like(sums_ref)
        up_sums_ref[...] = jnp.zeros_like(up_sums_ref)
        for group in (copies[2], copies[1], copies[0]):
            start_copies(group)
        for group in (copies[2], copies[1], copies[0]):
            wait_copies(group)

    width = w_down.shape[1]
    dnormed = dfinal_ref[...]
    for at in range(w_up.shape[1] // width):
        span = slice(at * width, at * width + width)
        dactive = dot_t(dbranch_ref[...], w_down[span, :])
        dhidden = (dactive * slope_ref[:, span].astype(F32)).astype(BF)
        dhidden_ref[:, span] = dhidden
        up_sums_ref[:, span] += jnp.sum(dhidden.astype(F32), axis=0, keepdims=True)
        dnormed = dnormed + dot_t(dhidden, w_up[:, span])
    hat, scale = norm_parts(resid_ref[...])
    dresid = norm_back(dnormed * small_ref[1:2, :], hat, scale)
    dresid_ref[...] = dresid
    dattn = dresid.astype(BF)
    dattn_ref[...] = dattn
    dmixed_ref[...] = dot_t(dattn, w_out[...]).astype(BF)
    add_rows(sums_ref, (dnormed * hat, dnormed, dattn))


def backward(index, parts, dbranch, slope, dfinal, resid, smalls, block=256):
    rows, width = resid.shape
    hidden = slope.shape[1]
    narrow = pl.BlockSpec((block, width), lambda i: (i, 0))
    wide = pl.BlockSpec((block, hidden), lambda i: (i, 0))
    whole = lambda a: pl.BlockSpec(a.shape, lambda i: (0, 0))
    return pl.pallas_call(
        backward_kernel,
        grid=(rows // block,),
        in_specs=[SMEM]
        + [ANY] * (3 * PARTS)
        + [narrow, wide, narrow, narrow, whole(smalls)],
        out_specs=[
            wide, narrow, narrow, narrow,
            pl.BlockSpec((8, width), lambda i: (0, 0)),
            pl.BlockSpec((1, hidden), lambda i: (0, 0)),
        ],
        out_shape=[
            struct((rows, hidden), BF),
            struct((rows, width), F32),
            struct((rows, width), BF),
            struct((rows, width), BF),
            struct((8, width), F32),
            struct((1, hidden), F32),
        ],
        scratch_shapes=[
            pltpu.VMEM((width, width), BF),
            pltpu.VMEM((width, hidden), BF),
            pltpu.VMEM((hidden, width), BF),
            pltpu.SemaphoreType.DMA((3, PARTS)),
        ],
        compiler_params=params(),
        cost_estimate=cost(2 * rows * width * (width + 2 * hidden), 40e6),
        name="backward",
    )(index, *parts[0], *parts[1], *parts[2], dbranch, slope, dfinal, resid, smalls)


def rows_kernel(index, left_ref, *refs):
    count = (len(refs) - 3) // 1
    rights, (keep_ref, send_ref, total) = refs[:count], refs[count:]
    right = jnp.concatenate([ref[...] for ref in rights], axis=1)
    total[...] = tdot(left_ref[...], right).astype(BF).reshape(total.shape)
    me = index[0]
    keep_ref[0] = total[me]
    keep_ref[1] = total[me ^ 2]
    send_ref[0] = total[me ^ 1]
    send_ref[1] = total[me ^ 3]


def weight_rows(index, left, rights, block=None):
    tokens, width = left.shape
    columns = sum(right.shape[1] for right in rights)
    block = block or columns
    shard = width // 4
    if len(rights) == 1:
        right_specs = [pl.BlockSpec((tokens, block), lambda i: (0, i))]
    else:
        right_specs = [pl.BlockSpec(right.shape, lambda i: (0, 0)) for right in rights]
    out = pl.BlockSpec((2, shard, block), lambda i: (0, 0, i))
    return pl.pallas_call(
        rows_kernel,
        grid=(columns // block,),
        in_specs=[SMEM, pl.BlockSpec((tokens, width), lambda i: (0, 0))] + right_specs,
        out_specs=[out, out],
        out_shape=[struct((2, shard, columns), BF)] * 2,
        scratch_shapes=[pltpu.VMEM((4, shard, block), BF)],
        compiler_params=params(),
        cost_estimate=cost(2 * tokens * width * columns, 4 * width * columns),
        name="weight_rows",
    )(index, left, *rights)


def down_kernel(index, left_ref, right_ref, send_ref, keep_ref):
    del index
    total = tdot(left_ref[...], right_ref[...]).astype(BF)

    @pl.when(pl.program_id(0) < 2)
    def _():
        send_ref[0] = total

    @pl.when(pl.program_id(0) >= 2)
    def _():
        keep_ref[0] = total


def down_rows(index, left, right):
    tokens, hidden = left.shape
    width = right.shape[1]
    shard = hidden // 4
    block = lambda i, s: (0, s[0] ^ jnp.where(i < 2, 2 * i + 1, 2 * i - 4))
    out = lambda shift: lambda i, s: (jnp.clip(i - shift, 0, 1), 0, 0)
    send, keep = pl.pallas_call(
        down_kernel,
        grid_spec=pltpu.PrefetchScalarGridSpec(
            num_scalar_prefetch=1,
            grid=(4,),
            in_specs=[
                pl.BlockSpec((tokens, shard), block),
                pl.BlockSpec((tokens, width), lambda i, s: (0, 0)),
            ],
            out_specs=[
                pl.BlockSpec((1, shard, width), out(0)),
                pl.BlockSpec((1, shard, width), out(2)),
            ],
        ),
        out_shape=[struct((2, shard, width), BF)] * 2,
        compiler_params=params(),
        cost_estimate=cost(2 * tokens * width * hidden, 13e6),
        name="down_rows",
    )(index, left, right)
    return keep, send


def on_device(
    tokens,
    layout_cells,
    pad_mask,
    query_weight,
    key_weight,
    value_weight,
    out_weight,
    query_bias,
    value_bias,
    out_bias,
    bias_table,
    first_gain,
    first_shift,
    up_weight,
    up_bias,
    down_weight,
    down_bias,
    second_gain,
    second_shift,
    cotangent,
):
    rows, width = tokens.shape
    hidden = down_weight.shape[0] * 4
    shard = width // 4
    me = lax.axis_index("fsdp")
    parity = lax.axis_index("dp") & 1
    index = jnp.stack([me, parity]).astype(jnp.int32)
    factor = 1.0 / math.sqrt(rows * lax.axis_size("dp") * lax.axis_size("fsdp"))

    vectors = (
        query_bias, value_bias, out_bias, first_gain, first_shift, down_bias, second_gain,
        second_shift,
    )
    table_row = jnp.pad(bias_table.reshape(-1), (0, width - bias_table.size))
    pack = jnp.concatenate(vectors + (up_bias, table_row)).reshape(4, width)
    packs = jnp.stack([pack, swap(pack, "fsdp", 1), swap(pack, "fsdp", 2), swap(pack, "fsdp", 3)])
    packs = jnp.stack(
        [lax.dynamic_index_in_dim(packs, me ^ at, 0, keepdims=False) for at in range(4)]
    )
    full_vectors = packs[:, :2].reshape(4, 8, shard).transpose(1, 0, 2).reshape(8, width)
    full_vectors = full_vectors.astype(F32)
    full_up_bias = packs[:, 2].reshape(1, hidden).astype(F32)
    table = packs[:, 3, : bias_table.size].reshape(HEADS, 3 * BUCKETS)
    smalls = full_vectors[2:8]

    qkv_parts = gather(jnp.concatenate([query_weight, key_weight, value_weight], axis=1), parity)
    out_parts = gather(out_weight, parity)
    up_parts = gather(up_weight, parity)
    down_parts = gather(down_weight, parity)

    extra, ke, ket, oh, near, near_t = prepare(layout_cells, pad_mask, table)
    qkv = project(index, qkv_parts, tokens, full_vectors[:2])
    mixed, extra = attend(qkv, extra, ket, near)
    weights = (out_parts, up_parts, down_parts)
    result, dfinal, dbranch, active, slope, normed, resid, sums_two = forward(
        index, weights, mixed, tokens, cotangent, smalls, full_up_bias
    )
    down_grad = down_rows(index, active, dbranch)
    dhidden, dresid, dattn, dmixed, sums_one, up_sums = backward(
        index, weights, dbranch, slope, dfinal, resid, smalls
    )
    up_grad = weight_rows(index, normed, (dhidden,), 768)
    out_grad = weight_rows(index, mixed, (dattn,))
    grad_down = reduce_rows(*down_grad, factor)
    grad_up = reduce_rows(*up_grad, factor)
    grad_out = reduce_rows(*out_grad, factor)

    grads, fars, nears, totals = [], [], [], []
    for group in GROUPS:
        dq, dk, dv, far, near_sums = attend_back(
            group, qkv, extra, ke, ket, oh, near_t, dmixed, mixed
        )
        grads += [dq, dk, dv]
        fars.append(far)
        nears.append(near_sums)
        totals.append(reduce_rows(*weight_rows(index, tokens, (dq, dk, dv)), factor))
    thirds = [[] for _ in range(3)]
    for total in totals:
        for at, piece in enumerate(jnp.split(total, 3, axis=1)):
            thirds[at].append(piece)
    grad_query, grad_key, grad_value = (jnp.concatenate(third, axis=1) for third in thirds)
    input_grad = input_gradient(index, qkv_parts, grads, dresid)

    table_grad = table_gradient(jnp.concatenate(fars), jnp.concatenate(nears))
    column_sum = lambda arrays: jnp.concatenate(
        [jnp.sum(a, axis=0, dtype=F32) for a in arrays]
    )
    sums = jnp.stack(
        [
            column_sum(grads[0::3]),
            column_sum(grads[2::3]),
            sums_one[2],
            sums_one[0],
            sums_one[1],
            sums_two[2],
            sums_two[0],
            sums_two[1],
        ]
    )
    sums, up_sums, table_grad = lax.psum((sums, up_sums, table_grad), ("dp", "fsdp"))
    sums = lax.dynamic_slice_in_dim(sums, me * shard, shard, 1) * factor
    up_sums = lax.dynamic_slice_in_dim(up_sums[0], me * (hidden // 4), hidden // 4, 0) * factor
    table_grad = lax.dynamic_slice_in_dim(table_grad, me * (HEADS // 4), HEADS // 4, 0) * factor
    return (
        result,
        input_grad,
        grad_query,
        grad_key,
        grad_value,
        grad_out,
        sums[0],
        sums[1],
        sums[2],
        table_grad,
        sums[3],
        sums[4],
        grad_up,
        up_sums,
        grad_down,
        sums[5],
        sums[6],
        sums[7],
    )


def solution(mesh):
    rows = P(("dp", "fsdp"), None)
    matrix, vector = P("fsdp", None), P("fsdp")
    return jax.shard_map(
        on_device,
        mesh=mesh,
        in_specs=(
            rows, P(None, ("dp", "fsdp")), P(("dp", "fsdp")),
            matrix, matrix, matrix, matrix,
            vector, vector, vector, matrix, vector, vector,
            matrix, vector, matrix, vector, vector, vector,
            rows,
        ),
        out_specs=(
            rows, rows,
            matrix, matrix, matrix, matrix,
            vector, vector, vector, matrix, vector, vector,
            matrix, vector, matrix, vector, vector, vector,
        ),
        check_vma=False,
    )
```

time: 1280 us -> 514 us (0.40)
  matrix products: 304 us -> 1.78 us
  blocking collectives: 343 us -> 41.8 us
  local copies, waits for them, and re-layouts: 300 us -> 20.3 us
  Pallas kernels: 0 us -> 190 us
  other arithmetic: 155 us -> 21.1 us
  starting transfers between devices: 0.47 us -> 68.2 us
  waiting for transfers between devices: 120 us -> 159 us
  loops' own time: 28.6 us -> 0 us
  between operations: 18.6 us -> 1.97 us
    dot_general x38 -> x2, matrix products: 304 us -> 1.78 us  [the longest x1 1.6 us: table_gradient(): jnp.dot(sums, pick, precision=lax.Precision.HIGHEST, preferred_element_ty...]
    psum x1, blocking collectives: 309 us -> 41.8 us  [on_device(): lax.psum((sums, up_sums, table_grad), ('dp', 'fsdp'))]
    pallas_call x0 -> x15, Pallas kernels: none -> 190 us  [the longest x3 46 us: attend_back(): pl.pallas_call(attend_back_kernel, grid=(pairs, windows), in_specs=[block...]
    ppermute x0 -> x65, waiting for transfers between devices: none -> 159 us  [swap(): lax.ppermute(array, axis, [(i, i ^ bit) for i in range(lax.axis_size(axis...]
    while x76 -> x0, local copies, waits for them, and re-layouts: 131 us -> none
    reshape x12 -> x3, local copies, waits for them, and re-layouts: 101 us -> 0.75 us  [the longest x1 0.65 us: prepare(): jnp.dot(table, pick, preferred_element_type=F32).reshape(HEADS, 1, LANES)]
    reduce_scatter x2 -> x0, waiting for transfers between devices: 99 us -> none  [the longest x1 50.4 us: on_device(): lax.psum_scatter(grad_down.astype(jnp.bfloat16), 'fsdp', scatter_dimensio...]
    ppermute x0 -> x65, starting transfers between devices: none -> 68.2 us  [swap(): lax.ppermute(array, axis, [(i, i ^ bit) for i in range(lax.axis_size(axis...]
  transfers between devices with their start and end apart: 12 -> 65, of which waited for: 4 -> 29; matrix products, arithmetic and copies ran while one was open for 53% -> 7% of each run, Pallas kernels for 0% -> 17%
where the time goes in v1:
time: 514 us; the launch traced here: 504 us
  Pallas kernels  190 us (37%)
  waiting for transfers between devices  159 us (31%)
  starting transfers between devices  68.2 us (13%)
  blocking collectives  41.8 us (8%)
  other arithmetic  21.1 us (4%)
  local copies, waits for them, and re-layouts  20.3 us (4%)
    ppermute x65, waiting for transfers between devices, swap(): lax.ppermute(array, axis, [(i, i ^ bit) for i in range(lax.axis_size(axis...  159 us
    ppermute x65, starting transfers between devices, swap(): lax.ppermute(array, axis, [(i, i ^ bit) for i in range(lax.axis_size(axis...  68.2 us
    pallas_call x3, Pallas kernels, attend_back(): pl.pallas_call(attend_back_kernel, grid=(pairs, windows), in_specs=[block...  46 us
    psum x1, blocking collectives, on_device(): lax.psum((sums, up_sums, table_grad), ('dp', 'fsdp'))  41.8 us
    pallas_call x1, Pallas kernels, attend(): pl.pallas_call(attend_kernel, grid=(PAIRS, windows), in_specs=[head_block...  31.8 us
    pallas_call x5, Pallas kernels, weight_rows(): pl.pallas_call(rows_kernel, grid=(columns // block,), in_specs=[SMEM, pl....  27 us
    pallas_call x1, Pallas kernels, forward(): pl.pallas_call(forward_kernel, grid=(rows // block,), in_specs=[SMEM] + [...  24.9 us
    pallas_call x1, Pallas kernels, backward(): pl.pallas_call(backward_kernel, grid=(rows // block,), in_specs=[SMEM] +...  21.8 us
  transfers between devices with their start and end apart: 65, of which 29 were waited for; matrix products, arithmetic and copies ran while one was open for 7% of the time, Pallas kernels for 17%

profile of v1, /device:TPU:0, one launch (start us, length us, event | category | flops | bytes accessed | tf_op | source)
XLA Modules:
  0.0 503.8 jit_solution(8618493632075693729)
XLA Ops:
  1.9 3.0 collective-permute-start.6
  5.4 2.1 collective-permute-start.16
  7.4 14.9 %collective-permute-done.1.refs_2_ = bf16[96,768]{1,0:T(8,128)(2,1)} collective-permute-done((bf16[96,768]{1,0:T(8,128)(2,1)S(1)}, bf16[96,768]{1,0:T(8,128)(2,1)}, u32[]{:S(2)}, u32[]{:S(2)}) %collective-permute-start.1) | collective-permute-done | bytes 147488 | tf_op jit(solution)/shard_map/ppermute | solution.py:59
  22.4 2.0 collective-permute-start.2
  26.1 1.5 collective-permute-start.21
  27.6 3.5 collective-permute-done.21
  31.5 2.7 collective-permute-done.22
  43.1 9.4 %collective-permute-done.11.refs_14_ = bf16[384,768]{1,0:T(8,128)(2,1)} collective-permute-done((bf16[384,768]{1,0:T(8,128)(2,1)S(1)}, bf16[384,768]{1,0:T(8,128)(2,1)}, u32[]{:S(2)}, u32[]{:S(2)}) %collective-permute-start.11) | collective-permute-done | bytes 589856 | tf_op jit(solution)/shard_map/ppermute | solution.py:59
  52.6 1.8 collective-permute-start.12
  55.0 9.6 %collective-permute-done.7.refs_9_ = bf16[96,3072]{1,0:T(8,128)(2,1)} collective-permute-done((bf16[96,3072]{1,0:T(8,128)(2,1)S(1)}, bf16[96,3072]{1,0:T(8,128)(2,1)}, u32[]{:S(2)}, u32[]{:S(2)}) %collective-permute-start.7) | collective-permute-done | bytes 589856 | tf_op jit(solution)/shard_map/ppermute | solution.py:59
  67.7 9.5 %prepare.1 = (bf16[1024,1536]{1,0:T(8,128)(2,1)}, bf16[1024,128]{1,0:T(8,128)(2,1)}, bf16[128,1024]{1,0:T(8,128)(2,1)}, bf16[1024,128]{1,0:T(8,128)(2,1)}, f32[1...) custom-call(s32[1024,4]{1,0:T(8,128)} %copy.53.cols_ref, s32[4,1024]{1,0:T(4,128)} %get-tuple-element.147.rows_ref, ...), custom_call_target="tpu_custom_call" | custom-call | flops 402653184 | bytes 7000000 | tf_op jit(solution)/shard_map/prepare/pallas_call | solution.py:222
  78.3 8.9 %project.1.q_ref.k_ref.v_ref = bf16[1024,2304]{1,0:T(8,128)(2,1)} custom-call(s32[2]{0:T(128)} %pad_add_fusion.index, bf16[192,2304]{1,0:T(8,128)(2,1)} %copy-done.7, bf16[192,2304]{1,0:T(8,128)(2,1)} %collective-permute-done.15.refs_1_, bf16[96,2304]{1,0:T(8,128)(2,1)} %collective-permute-done.16.refs_2_, bf16[96,2304]{1,0:T(8,128)(2,1)} %copy-done.48, ...), custom_call_target="tpu_custom_call" | custom-call | flops 3623878656 | bytes 10000000 | tf_op jit(solution)/shard_map/project/pallas_call | solution.py:277
  87.2 31.8 %attend.1 = (bf16[1024,768]{1,0:T(8,128)(2,1)}, bf16[1024,1536]{1,0:T(8,128)(2,1)}) custom-call(bf16[1024,2304]{1,0:T(8,128)(2,1)} %project.1.q_ref.k_ref.v_ref, bf16[1024,2304]{1,0:T(8,128)(2,1)} %project.1.q_ref.k_ref.v_ref, bf16[1024,2304]{1,0:T(8,128)(2,1)} %project.1.q_ref.k_ref.v_ref, bf16[1024,1536]{1,0:T(8,128)(2,1)} %get-tuple-element.67.e_ref, ...), custom_call_target="tpu_custom_call" | custom-call | flops 4831838208 | bytes 17000000 | tf_op jit(solution)/shard_map/attend/pallas_call | solution.py:385
  120.6 24.9 %forward.1 = (bf16[1024,768]{1,0:T(8,128)(2,1)}, f32[1024,768]{1,0:T(8,128)}, bf16[1024,768]{1,0:T(8,128)(2,1)}, bf16[1024,3072]{1,0:T(8,128)(2,1)}, bf16[1024,3...) custom-call(s32[2]{0:T(128)} %pad_add_fusion.index, ...), custom_call_target="tpu_custom_call" | custom-call | flops 10871635968 | bytes 40000000 | tf_op jit(solution)/shard_map/forward/pallas_call | solution.py:663
  145.5 21.8 %backward.1 = (bf16[1024,3072]{1,0:T(8,128)(2,1)}, f32[1024,768]{1,0:T(8,128)}, bf16[1024,768]{1,0:T(8,128)(2,1)}, bf16[1024,768]{1,0:T(8,128)(2,1)}, f32[8,768]{1,0:T(8,128)}, /*index=5*/f32[1,3072]{1,0:T(1,128)}) custom-call(s32[2]{0:T(128)} %pad_add_fusion.index, bf16[192,768]{1,0:T(8,128)(2,1)} %refs_0_.3, ...), custom_call_target="tpu_custom_call" | custom-call | flops 10871635968 | bytes 40000000 | tf_op jit(solution)/shard_map/backward/pallas_call | solution.py:739
  167.2 15.6 %attend_back.5 = (bf16[1024,256]{1,0:T(8,128)(2,1)}, bf16[1024,256]{1,0:T(8,128)(2,1)}, bf16[1024,256]{1,0:T(8,128)(2,1)}, f32[4,8,128]{2,1,0:T(8,128)}, f32[4,8,256]{2,1,0:T(8,128)}) custom-call(bf16[1024,2304]{1,0:T(8,128)(2,1)} %project.1.q_ref.k_ref.v_ref, bf16[1024,2304]{1,0:T(8,128)(2,1)} %project.1.q_ref.k_ref.v_ref, ...), custom_call_target="tpu_custom_call" | custom-call | flops 4294967296 | bytes 12000000 | tf_op jit(solution)/shard_map/attend_back/pallas_call | solution.py:513
  182.9 15.2 %attend_back.4 = (bf16[1024,256]{1,0:T(8,128)(2,1)}, bf16[1024,256]{1,0:T(8,128)(2,1)}, bf16[1024,256]{1,0:T(8,128)(2,1)}, f32[4,8,128]{2,1,0:T(8,128)}, f32[4,8,256]{2,1,0:T(8,128)}) custom-call(bf16[1024,2304]{1,0:T(8,128)(2,1)} %project.1.q_ref.k_ref.v_ref, bf16[1024,2304]{1,0:T(8,128)(2,1)} %project.1.q_ref.k_ref.v_ref, ...), custom_call_target="tpu_custom_call" | custom-call | flops 4294967296 | bytes 12000000 | tf_op jit(solution)/shard_map/attend_back/pallas_call | solution.py:513
  198.1 15.1 %attend_back.3 = (bf16[1024,256]{1,0:T(8,128)(2,1)}, bf16[1024,256]{1,0:T(8,128)(2,1)}, bf16[1024,256]{1,0:T(8,128)(2,1)}, f32[4,8,128]{2,1,0:T(8,128)}, f32[4,8,256]{2,1,0:T(8,128)}) custom-call(bf16[1024,2304]{1,0:T(8,128)(2,1)} %project.1.q_ref.k_ref.v_ref, bf16[1024,2304]{1,0:T(8,128)(2,1)} %project.1.q_ref.k_ref.v_ref, ...), custom_call_target="tpu_custom_call" | custom-call | flops 4294967296 | bytes 12000000 | tf_op jit(solution)/shard_map/attend_back/pallas_call | solution.py:513
  213.3 10.6 %down_rows.1 = (bf16[2,768,768]{2,1,0:T(8,128)(2,1)}, bf16[2,768,768]{2,1,0:T(8,128)(2,1)}) custom-call(s32[2]{0:T(128)} %pad_add_fusion.index, bf16[1024,3072]{1,0:T(8,128)(2,1)} %get-tuple-element.113.left_ref, bf16[1024,768]{1,0:T(8,128)(2,1)} %get-tuple-element.76.refs_18_.right_ref), custom_call_target="tpu_custom_call" | custom-call | flops 4831838208 | bytes 13000000 | tf_op jit(solution)/shard_map/down_rows/pallas_call | solution.py:824
  224.0 9.4 %weight_rows.9 = (bf16[2,192,3072]{2,1,0:T(8,128)(2,1)}, bf16[2,192,3072]{2,1,0:T(8,128)(2,1)}) custom-call(s32[2]{0:T(128)} %pad_add_fusion.index, bf16[1024,768]{1,0:T(8,128)(2,1)} %get-tuple-element.108.left_ref, bf16[1024,3072]{1,0:T(8,128)(2,1)} %get-tuple-element.109.refs_0_), custom_call_target="tpu_custom_call" | custom-call | flops 4831838208 | bytes 9437184 | tf_op jit(solution)/shard_map/weight_rows/pallas_call | solution.py:792
  233.9 4.5 weight_rows.8
  239.3 4.4 weight_rows.5
  244.1 1.8 convert_reduce_fusion.1
  245.9 4.4 weight_rows.6
  250.3 1.8 convert_reduce_fusion
  252.8 1.6 fusion.7
  254.4 9.7 %input_gradient.1 = bf16[1024,768]{1,0:T(8,128)(2,1)} custom-call(s32[2]{0:T(128)} %pad_add_fusion.index, bf16[192,2304]{1,0:T(8,128)(2,1)} %copy-done.7, bf16[192,2304]{1,0:T(8,128)(2,1)} %collective-permute-done.15.refs_1_, bf16[96,2304]{1,0:T(8,128)(2,1)} %collective-permute-done.16.refs_2_, bf16[96,2304]{1,0:T(8,128)(2,1)} %copy-done.48, ...), custom_call_target="tpu_custom_call" | custom-call | flops 3623878656 | bytes 13000000 | tf_op jit(solution)/shard_map/input_gradient/pallas_call | solution.py:317
  270.8 41.8 %all-reduce.1 = (f32[8,768]{1,0:T(8,128)}, f32[12,96]{1,0:T(8,128)}, f32[1,3072]{1,0:T(1,128)S(1)}) all-reduce(f32[8,768]{1,0:T(8,128)} %stack.48, f32[12,96]{1,0:T(8,128)} %fusion.7, f32[1,3072]{1,0:T(1,128)} %get-tuple-element.112), channel_id=1, replica_groups=mesh['dp'=8,'fsdp'=4] {'dp','fsdp'}, use_global_device_ids=true, to_apply=%region_6.7 | all-reduce | flops 10368 | bytes 82944 | tf_op jit(solution)/shard_map/psum | solution.py:946
  312.6 4.3 weight_rows.7
  324.4 2.4 collective-permute-start.45
  327.0 2.1 collective-permute-start.31
  329.2 5.4 %collective-permute-done.45 = bf16[192,768]{1,0:T(8,128)(2,1)S(1)} collective-permute-done((bf16[192,768]{1,0:T(8,128)(2,1)S(1)}, bf16[192,768]{1,0:T(8,128)(2,1)S(1)}, u32[]{:S(2)}, u32[]{:S(2)}) %collective-permute-start.45) | collective-permute-done | bytes 294944 | tf_op jit(solution)/shard_map/ppermute | solution.py:59
  334.6 2.0 collective-permute-start.38
  336.7 4.2 collective-permute-done.24
  340.9 1.9 collective-permute-start.46
  343.0 4.3 collective-permute-done.31
  347.2 1.9 collective-permute-start.25
  349.3 3.9 collective-permute-done.38
  353.2 1.7 collective-permute-start.32
  355.4 1.6 collective-permute-start.47
  357.0 2.9 collective-permute-done.32
  365.1 2.3 collective-permute-start.48
  367.4 2.0 collective-permute-start.27
  370.6 1.6 fusion.1
  372.2 1.8 collective-permute-start.59
  374.8 2.0 collective-permute-start.41
  379.5 1.6 collective-permute-done.41
  384.5 16.6 %collective-permute-done.59 = bf16[768,768]{1,0:T(8,128)(2,1)S(1)} collective-permute-done((bf16[768,768]{1,0:T(8,128)(2,1)S(1)}, bf16[768,768]{1,0:T(8,128)(2,1)S(1)}, u32[]{:S(2)}, u32[]{:S(2)}) %collective-permute-start.59) | collective-permute-done | bytes 1179680 | tf_op jit(solution)/shard_map/ppermute | solution.py:59
  401.2 1.7 collective-permute-start.50
  403.3 18.9 %collective-permute-done.52 = bf16[192,3072]{1,0:T(8,128)(2,1)S(1)} collective-permute-done((bf16[192,3072]{1,0:T(8,128)(2,1)S(1)}, bf16[192,3072]{1,0:T(8,128)(2,1)S(1)}, u32[]{:S(2)}, u32[]{:S(2)}) %collective-permute-start.52) | collective-permute-done | bytes 1179680 | tf_op jit(solution)/shard_map/ppermute | solution.py:59
  427.2 25.1 %collective-permute-done.29 = bf16[96,768]{1,0:T(8,128)(2,1)S(1)} collective-permute-done((bf16[96,768]{1,0:T(8,128)(2,1)S(1)}, bf16[96,768]{1,0:T(8,128)(2,1)S(1)}, u32[]{:S(2)}, u32[]{:S(2)}) %collective-permute-start.29) | collective-permute-done | bytes 147488 | tf_op jit(solution)/shard_map/ppermute | solution.py:59
  452.8 2.0 collective-permute-start.61
  455.1 7.2 %collective-permute-done.61 = bf16[192,768]{1,0:T(8,128)(2,1)S(1)} collective-permute-done((bf16[192,768]{1,0:T(8,128)(2,1)S(1)}, bf16[192,768]{1,0:T(8,128)(2,1)S(1)}, u32[]{:S(2)}, u32[]{:S(2)}) %collective-permute-start.61) | collective-permute-done | bytes 294944 | tf_op jit(solution)/shard_map/ppermute | solution.py:59
  462.4 3.4 collective-permute-start.62
  465.7 5.9 %collective-permute-done.54 = bf16[48,3072]{1,0:T(8,128)(2,1)S(1)} collective-permute-done((bf16[48,3072]{1,0:T(8,128)(2,1)S(1)}, bf16[48,3072]{1,0:T(8,128)(2,1)S(1)}, u32[]{:S(2)}, u32[]{:S(2)}) %collective-permute-start.54) | collective-permute-done | bytes 294944 | tf_op jit(solution)/shard_map/ppermute | solution.py:59
  473.3 1.6 collective-permute-done.62
  475.0 3.4 collective-permute-start.63
  478.3 5.1 %collective-permute-done.55 = bf16[48,3072]{1,0:T(8,128)(2,1)S(1)} collective-permute-done((bf16[48,3072]{1,0:T(8,128)(2,1)S(1)}, bf16[48,3072]{1,0:T(8,128)(2,1)S(1)}, u32[]{:S(2)}, u32[]{:S(2)}) %collective-permute-start.55) | collective-permute-done | bytes 294944 | tf_op jit(solution)/shard_map/ppermute | solution.py:59
  485.1 1.8 collective-permute-start.64
  487.0 3.3 collective-permute-done.56
  490.4 1.8 collective-permute-start.57
  495.5 1.7 convert_multiply_fusion
  497.2 4.6 collective-permute-done.57
  501.9 1.7 convert_multiply_fusion.1
  (304 shorter events, 62.9 us)
Async XLA Ops:
  1.9 38.3 %collective-permute-start.6 = (bf16[96,3072]{1,0:T(8,128)(2,1)S(1)}, bf16[96,3072]{1,0:T(8,128)(2,1)S(1)}, u32[]{:S(2)}, u32[]{:S(2)}) collective-permute-start(bf16[96,3072]{1,0:T(8,128)(2,1)S(1)} %constant_dynamic-slice_fusion.9), channel_id=1, source_target_pairs={{0,2},{1,3},{2,0},{3,1},{4,6},{5,7},{6,4},{7,5},{8,10},{9,11},{10,... | collective-permute-start | bytes 1769480 | tf_op jit(solution)/shard_map/ppermute | solution.py:59
  5.0 17.4 %collective-permute-start.1 = (bf16[96,768]{1,0:T(8,128)(2,1)S(1)}, bf16[96,768]{1,0:T(8,128)(2,1)}, u32[]{:S(2)}, u32[]{:S(2)}) collective-permute-start(bf16[96,768]{1,0:T(8,128)(2,1)S(1)} %constant_dynamic-slice_fusion.10), channel_id=1, source_target_pairs={{0,2},{1,3},{2,0},{3,1},{4,6},{5,7},{6,4},{7,5},{8,10},{9,11},{10,... | collective-permute-start | bytes 442376 | tf_op jit(solution)/shard_map/ppermute | solution.py:59
  5.4 33.3 %collective-permute-start.16 = (bf16[96,2304]{1,0:T(8,128)(2,1)S(1)}, bf16[96,2304]{1,0:T(8,128)(2,1)}, u32[]{:S(2)}, u32[]{:S(2)}) collective-permute-start(bf16[96,2304]{1,0:T(8,128)(2,1)S(1)} %constant_dynamic-slice_fusion.7), channel_id=1, source_target_pairs={{0,2},{1,3},{2,0},{3,1},{4,6},{5,7},{6,4},{7,5},{8,10},{9,11},{10,... | collective-permute-start | bytes 1327112 | tf_op jit(solution)/shard_map/ppermute | solution.py:59
  22.4 11.9 %collective-permute-start.2 = (bf16[96,768]{1,0:T(8,128)(2,1)}, bf16[96,768]{1,0:T(8,128)(2,1)}, u32[]{:S(2)}, u32[]{:S(2)}) collective-permute-start(bf16[96,768]{1,0:T(8,128)(2,1)} %collective-permute-done.1.refs_2_), channel_id=1, source_target_pairs={{0,4},{4,0},{8,12},{12,8},{16,20},{20,16},{24,28},{28,24},{1,5},{5... | collective-permute-start | bytes 442376 | tf_op jit(solution)/shard_map/ppermute | solution.py:59
  24.4 14.2 %collective-permute-start = (bf16[192,768]{1,0:T(8,128)(2,1)S(1)}, bf16[192,768]{1,0:T(8,128)(2,1)}, u32[]{:S(2)}, u32[]{:S(2)}) collective-permute-start(bf16[192,768]{1,0:T(8,128)(2,1)S(1)} %copy-done.19), channel_id=1, source_target_pairs={{0,1},{1,0},{2,3},{3,2},{4,5},{5,4},{6,7},{7,6},{8,9},{9,8},{10,11... | collective-permute-start | bytes 884744 | tf_op jit(solution)/shard_map/ppermute | solution.py:59
  26.1 5.0 collective-permute-start.21
  31.1 3.1 collective-permute-start.22
  34.1 20.5 %collective-permute-start.15 = (bf16[192,2304]{1,0:T(8,128)(2,1)S(1)}, bf16[192,2304]{1,0:T(8,128)(2,1)}, u32[]{:S(2)}, u32[]{:S(2)}) collective-permute-start(bf16[192,2304]{1,0:T(8,128)(2,1)S(1)} %constant_dynamic-update-slice_fusion.refs_0_), channel_id=1, source_target_pairs={{0,1},{1,0},{2,3},{3,2},{4,5},{5,4},{6,7},{7,6},{8,9},{9,8},{10,11... | collective-permute-start | bytes 2654216 | tf_op jit(solution)/shard_map/ppermute | solution.py:59
  34.3 2.9 collective-permute-start.3
  37.1 15.5 %collective-permute-start.11 = (bf16[384,768]{1,0:T(8,128)(2,1)S(1)}, bf16[384,768]{1,0:T(8,128)(2,1)}, u32[]{:S(2)}, u32[]{:S(2)}) collective-permute-start(bf16[384,768]{1,0:T(8,128)(2,1)S(1)} %constant_dynamic-slice_fusion.8), channel_id=1, source_target_pairs={{0,2},{1,3},{2,0},{3,1},{4,6},{5,7},{6,4},{7,5},{8,10},{9,11},{10,... | collective-permute-start | bytes 1769480 | tf_op jit(solution)/shard_map/ppermute | solution.py:59
  38.6 3.8 collective-permute-start.4
  38.7 13.9 %collective-permute-start.17 = (bf16[96,2304]{1,0:T(8,128)(2,1)}, bf16[96,2304]{1,0:T(8,128)(2,1)S(1)}, u32[]{:S(2)}, u32[]{:S(2)}) collective-permute-start(bf16[96,2304]{1,0:T(8,128)(2,1)} %collective-permute-done.16.refs_2_), channel_id=1, source_target_pairs={{0,4},{4,0},{8,12},{12,8},{16,20},{20,16},{24,28},{28,24},{1,5},{5... | collective-permute-start | bytes 1327112 | tf_op jit(solution)/shard_map/ppermute | solution.py:59
  40.2 24.4 %collective-permute-start.7 = (bf16[96,3072]{1,0:T(8,128)(2,1)S(1)}, bf16[96,3072]{1,0:T(8,128)(2,1)}, u32[]{:S(2)}, u32[]{:S(2)}) collective-permute-start(bf16[96,3072]{1,0:T(8,128)(2,1)S(1)} %collective-permute-done.6.refs_8_), channel_id=1, source_target_pairs={{0,4},{4,0},{8,12},{12,8},{16,20},{20,16},{24,28},{28,24},{1,5},{5... | collective-permute-start | bytes 1769480 | tf_op jit(solution)/shard_map/ppermute | solution.py:59
  42.4 12.0 %collective-permute-start.18 = (bf16[96,2304]{1,0:T(8,128)(2,1)}, bf16[96,2304]{1,0:T(8,128)(2,1)}, u32[]{:S(2)}, u32[]{:S(2)}) collective-permute-start(bf16[96,2304]{1,0:T(8,128)(2,1)} %collective-permute-done.16.refs_2_), channel_id=1, source_target_pairs={{0,1},{1,0},{2,3},{3,2},{4,5},{5,4},{6,7},{7,6},{8,9},{9,8},{10,11... | collective-permute-start | bytes 1327112 | tf_op jit(solution)/shard_map/ppermute | solution.py:59
  52.6 24.6 %collective-permute-start.8 = (bf16[96,3072]{1,0:T(8,128)(2,1)S(1)}, bf16[96,3072]{1,0:T(8,128)(2,1)}, u32[]{:S(2)}, u32[]{:S(2)}) collective-permute-start(bf16[96,3072]{1,0:T(8,128)(2,1)S(1)} %collective-permute-done.6.refs_8_), channel_id=1, source_target_pairs={{0,1},{1,0},{2,3},{3,2},{4,5},{5,4},{6,7},{7,6},{8,9},{9,8},{10,11... | collective-permute-start | bytes 1769480 | tf_op jit(solution)/shard_map/ppermute | solution.py:59
  52.6 25.2 %collective-permute-start.12 = (bf16[384,768]{1,0:T(8,128)(2,1)}, bf16[384,768]{1,0:T(8,128)(2,1)}, u32[]{:S(2)}, u32[]{:S(2)}) collective-permute-start(bf16[384,768]{1,0:T(8,128)(2,1)} %collective-permute-done.11.refs_14_), channel_id=1, source_target_pairs={{0,4},{4,0},{8,12},{12,8},{16,20},{20,16},{24,28},{28,24},{1,5},{5... | collective-permute-start | bytes 1769480 | tf_op jit(solution)/shard_map/ppermute | solution.py:59
  54.4 64.6 %collective-permute-start.10 = (bf16[768,768]{1,0:T(8,128)(2,1)}, bf16[768,768]{1,0:T(8,128)(2,1)S(1)}, u32[]{:S(2)}, u32[]{:S(2)}) collective-permute-start(bf16[768,768]{1,0:T(8,128)(2,1)} %refs_12_.3), channel_id=1, source_target_pairs={{0,1},{1,0},{2,3},{3,2},{4,5},{5,4},{6,7},{7,6},{8,9},{9,8},{10,11... | collective-permute-start | bytes 3538952 | tf_op jit(solution)/shard_map/ppermute | solution.py:59
  54.7 64.3 %collective-permute-start.5 = (bf16[192,3072]{1,0:T(8,128)(2,1)}, bf16[192,3072]{1,0:T(8,128)(2,1)}, u32[]{:S(2)}, u32[]{:S(2)}) collective-permute-start(bf16[192,3072]{1,0:T(8,128)(2,1)} %refs_6_.5), channel_id=1, source_target_pairs={{0,1},{1,0},{2,3},{3,2},{4,5},{5,4},{6,7},{7,6},{8,9},{9,8},{10,11... | collective-permute-start | bytes 3538952 | tf_op jit(solution)/shard_map/ppermute | solution.py:59
  64.6 13.3 %collective-permute-start.19 = (bf16[96,2304]{1,0:T(8,128)(2,1)}, bf16[96,2304]{1,0:T(8,128)(2,1)}, u32[]{:S(2)}, u32[]{:S(2)}) collective-permute-start(bf16[96,2304]{1,0:T(8,128)(2,1)} %copy-done.48), channel_id=1, source_target_pairs={{0,1},{1,0},{2,3},{3,2},{4,5},{5,4},{6,7},{7,6},{8,9},{9,8},{10,11... | collective-permute-start | bytes 1327112 | tf_op jit(solution)/shard_map/ppermute | solution.py:59
  77.2 41.8 %collective-permute-start.13 = (bf16[384,768]{1,0:T(8,128)(2,1)}, bf16[384,768]{1,0:T(8,128)(2,1)S(1)}, u32[]{:S(2)}, u32[]{:S(2)}) collective-permute-start(bf16[384,768]{1,0:T(8,128)(2,1)} %collective-permute-done.11.refs_14_), channel_id=1, source_target_pairs={{0,1},{1,0},{2,3},{3,2},{4,5},{5,4},{6,7},{7,6},{8,9},{9,8},{10,11... | collective-permute-start | bytes 1769480 | tf_op jit(solution)/shard_map/ppermute | solution.py:59
  77.8 41.2 %collective-permute-start.9 = (bf16[96,3072]{1,0:T(8,128)(2,1)}, bf16[96,3072]{1,0:T(8,128)(2,1)S(1)}, u32[]{:S(2)}, u32[]{:S(2)}) collective-permute-start(bf16[96,3072]{1,0:T(8,128)(2,1)} %collective-permute-done.7.refs_9_), channel_id=1, source_target_pairs={{0,1},{1,0},{2,3},{3,2},{4,5},{5,4},{6,7},{7,6},{8,9},{9,8},{10,11... | collective-permute-start | bytes 1769480 | tf_op jit(solution)/shard_map/ppermute | solution.py:59
  77.9 41.2 %collective-permute-start.14 = (bf16[384,768]{1,0:T(8,128)(2,1)}, bf16[384,768]{1,0:T(8,128)(2,1)S(1)}, u32[]{:S(2)}, u32[]{:S(2)}) collective-permute-start(bf16[384,768]{1,0:T(8,128)(2,1)} %collective-permute-done.12.refs_15_), channel_id=1, source_target_pairs={{0,1},{1,0},{2,3},{3,2},{4,5},{5,4},{6,7},{7,6},{8,9},{9,8},{10,11... | collective-permute-start | bytes 1769480 | tf_op jit(solution)/shard_map/ppermute | solution.py:59
  223.9 145.6 %collective-permute-start.58 = (bf16[2,768,768]{2,1,0:T(8,128)(2,1)}, bf16[2,768,768]{2,1,0:T(8,128)(2,1)}, u32[]{:S(2)}, u32[]{:S(2)}) collective-permute-start(bf16[2,768,768]{2,1,0:T(8,128)(2,1)} %get-tuple-element.115), channel_id=1, source_target_pairs={{0,1},{1,0},{2,3},{3,2},{4,5},{5,4},{6,7},{7,6},{8,9},{9,8},{10,11... | collective-permute-start | bytes 7077896 | tf_op jit(solution)/shard_map/ppermute | solution.py:59
  233.3 138.8 %collective-permute-start.51 = (bf16[2,192,3072]{2,1,0:T(8,128)(2,1)}, bf16[2,192,3072]{2,1,0:T(8,128)(2,1)S(1)}, u32[]{:S(2)}, u32[]{:S(2)}) collective-permute-start(bf16[2,192,3072]{2,1,0:T(8,128)(2,1)} %get-tuple-element.111), channel_id=1, source_target_pairs={{0,1},{1,0},{2,3},{3,2},{4,5},{5,4},{6,7},{7,6},{8,9},{9,8},{10,11... | collective-permute-start | bytes 7077896 | tf_op jit(solution)/shard_map/ppermute | solution.py:59
  238.4 85.6 %collective-permute-start.44 = (bf16[2,192,768]{2,1,0:T(8,128)(2,1)}, bf16[2,192,768]{2,1,0:T(8,128)(2,1)S(1)}, u32[]{:S(2)}, u32[]{:S(2)}) collective-permute-start(bf16[2,192,768]{2,1,0:T(8,128)(2,1)} %get-tuple-element.99), channel_id=1, source_target_pairs={{0,1},{1,0},{2,3},{3,2},{4,5},{5,4},{6,7},{7,6},{8,9},{9,8},{10,11... | collective-permute-start | bytes 1769480 | tf_op jit(solution)/shard_map/ppermute | solution.py:59
  243.7 80.7 %collective-permute-start.23 = (bf16[2,192,768]{2,1,0:T(8,128)(2,1)}, bf16[2,192,768]{2,1,0:T(8,128)(2,1)S(1)}, u32[]{:S(2)}, u32[]{:S(2)}) collective-permute-start(bf16[2,192,768]{2,1,0:T(8,128)(2,1)} %get-tuple-element.92), channel_id=1, source_target_pairs={{0,1},{1,0},{2,3},{3,2},{4,5},{5,4},{6,7},{7,6},{8,9},{9,8},{10,11... | collective-permute-start | bytes 1769480 | tf_op jit(solution)/shard_map/ppermute | solution.py:59
  321.1 5.7 %collective-permute-start.30 = (bf16[2,192,768]{2,1,0:T(8,128)(2,1)S(1)}, bf16[2,192,768]{2,1,0:T(8,128)(2,1)S(1)}, u32[]{:S(2)}, u32[]{:S(2)}) collective-permute-start(bf16[2,192,768]{2,1,0:T(8,128)(2,1)S(1)} %copy-done.43), channel_id=1, source_target_pairs={{0,1},{1,0},{2,3},{3,2},{4,5},{5,4},{6,7},{7,6},{8,9},{9,8},{10,11... | collective-permute-start | bytes 1769480 | tf_op jit(solution)/shard_map/ppermute | solution.py:59
  324.0 3.0 collective-permute-start.37
  324.4 10.2 %collective-permute-start.45 = (bf16[192,768]{1,0:T(8,128)(2,1)S(1)}, bf16[192,768]{1,0:T(8,128)(2,1)S(1)}, u32[]{:S(2)}, u32[]{:S(2)}) collective-permute-start(bf16[192,768]{1,0:T(8,128)(2,1)S(1)} %fusion.11), channel_id=1, source_target_pairs={{0,2},{1,3},{2,0},{3,1},{4,6},{5,7},{6,4},{7,5},{8,10},{9,11},{10,... | collective-permute-start | bytes 884744 | tf_op jit(solution)/shard_map/ppermute | solution.py:59
  326.8 14.1 %collective-permute-start.24 = (bf16[192,768]{1,0:T(8,128)(2,1)S(1)}, bf16[192,768]{1,0:T(8,128)(2,1)S(1)}, u32[]{:S(2)}, u32[]{:S(2)}) collective-permute-start(bf16[192,768]{1,0:T(8,128)(2,1)S(1)} %fusion.8), channel_id=1, source_target_pairs={{0,2},{1,3},{2,0},{3,1},{4,6},{5,7},{6,4},{7,5},{8,10},{9,11},{10,... | collective-permute-start | bytes 884744 | tf_op jit(solution)/shard_map/ppermute | solution.py:59
  327.0 20.2 %collective-permute-start.31 = (bf16[192,768]{1,0:T(8,128)(2,1)S(1)}, bf16[192,768]{1,0:T(8,128)(2,1)S(1)}, u32[]{:S(2)}, u32[]{:S(2)}) collective-permute-start(bf16[192,768]{1,0:T(8,128)(2,1)S(1)} %fusion.9), channel_id=1, source_target_pairs={{0,2},{1,3},{2,0},{3,1},{4,6},{5,7},{6,4},{7,5},{8,10},{9,11},{10,... | collective-permute-start | bytes 884744 | tf_op jit(solution)/shard_map/ppermute | solution.py:59
  334.6 18.6 %collective-permute-start.38 = (bf16[192,768]{1,0:T(8,128)(2,1)S(1)}, bf16[192,768]{1,0:T(8,128)(2,1)S(1)}, u32[]{:S(2)}, u32[]{:S(2)}) collective-permute-start(bf16[192,768]{1,0:T(8,128)(2,1)S(1)} %fusion.10), channel_id=1, source_target_pairs={{0,2},{1,3},{2,0},{3,1},{4,6},{5,7},{6,4},{7,5},{8,10},{9,11},{10,... | collective-permute-start | bytes 884744 | tf_op jit(solution)/shard_map/ppermute | solution.py:59
  340.9 14.1 %collective-permute-start.46 = (bf16[96,768]{1,0:T(8,128)(2,1)S(1)}, bf16[96,768]{1,0:T(8,128)(2,1)S(1)}, u32[]{:S(2)}, u32[]{:S(2)}) collective-permute-start(bf16[96,768]{1,0:T(8,128)(2,1)S(1)} %get-tuple-element.124), channel_id=1, source_target_pairs={{0,4},{4,0},{8,12},{12,8},{16,20},{20,16},{24,28},{28,24},{1,5},{5... | collective-permute-start | bytes 442376 | tf_op jit(solution)/shard_map/ppermute | solution.py:59
  347.2 8.2 %collective-permute-start.25 = (bf16[96,768]{1,0:T(8,128)(2,1)S(1)}, bf16[96,768]{1,0:T(8,128)(2,1)S(1)}, u32[]{:S(2)}, u32[]{:S(2)}) collective-permute-start(bf16[96,768]{1,0:T(8,128)(2,1)S(1)} %get-tuple-element.126), channel_id=1, source_target_pairs={{0,4},{4,0},{8,12},{12,8},{16,20},{20,16},{24,28},{28,24},{1,5},{5... | collective-permute-start | bytes 442376 | tf_op jit(solution)/shard_map/ppermute | solution.py:59
  353.2 6.7 %collective-permute-start.32 = (bf16[96,768]{1,0:T(8,128)(2,1)S(1)}, bf16[96,768]{1,0:T(8,128)(2,1)S(1)}, u32[]{:S(2)}, u32[]{:S(2)}) collective-permute-start(bf16[96,768]{1,0:T(8,128)(2,1)S(1)} %get-tuple-element.128), channel_id=1, source_target_pairs={{0,4},{4,0},{8,12},{12,8},{16,20},{20,16},{24,28},{28,24},{1,5},{5... | collective-permute-start | bytes 442376 | tf_op jit(solution)/shard_map/ppermute | solution.py:59
  355.0 6.8 %collective-permute-start.39 = (bf16[96,768]{1,0:T(8,128)(2,1)S(1)}, bf16[96,768]{1,0:T(8,128)(2,1)S(1)}, u32[]{:S(2)}, u32[]{:S(2)}) collective-permute-start(bf16[96,768]{1,0:T(8,128)(2,1)S(1)} %get-tuple-element.130), channel_id=1, source_target_pairs={{0,4},{4,0},{8,12},{12,8},{16,20},{20,16},{24,28},{28,24},{1,5},{5... | collective-permute-start | bytes 442376 | tf_op jit(solution)/shard_map/ppermute | solution.py:59
  355.4 8.0 %collective-permute-start.47 = (bf16[48,768]{1,0:T(8,128)(2,1)S(1)}, bf16[48,768]{1,0:T(8,128)(2,1)S(1)}, u32[]{:S(2)}, u32[]{:S(2)}) collective-permute-start(bf16[48,768]{1,0:T(8,128)(2,1)S(1)} %add_convert_fusion.16), channel_id=1, source_target_pairs={{0,8},{4,12},{8,0},{12,4},{16,24},{20,28},{24,16},{28,20},{1,9},{5... | collective-permute-start | bytes 221192 | tf_op jit(solution)/shard_map/ppermute | solution.py:59
  359.9 5.1 %collective-permute-start.26 = (bf16[48,768]{1,0:T(8,128)(2,1)S(1)}, bf16[48,768]{1,0:T(8,128)(2,1)S(1)}, u32[]{:S(2)}, u32[]{:S(2)}) collective-permute-start(bf16[48,768]{1,0:T(8,128)(2,1)S(1)} %add_convert_fusion.28), channel_id=1, source_target_pairs={{0,8},{4,12},{8,0},{12,4},{16,24},{20,28},{24,16},{28,20},{1,9},{5... | collective-permute-start | bytes 221192 | tf_op jit(solution)/shard_map/ppermute | solution.py:59
  361.9 5.6 %collective-permute-start.33 = (bf16[48,768]{1,0:T(8,128)(2,1)S(1)}, bf16[48,768]{1,0:T(8,128)(2,1)S(1)}, u32[]{:S(2)}, u32[]{:S(2)}) collective-permute-start(bf16[48,768]{1,0:T(8,128)(2,1)S(1)} %add_convert_fusion.24), channel_id=1, source_target_pairs={{0,8},{4,12},{8,0},{12,4},{16,24},{20,28},{24,16},{28,20},{1,9},{5... | collective-permute-start | bytes 221192 | tf_op jit(solution)/shard_map/ppermute | solution.py:59
  363.4 11.0 %collective-permute-start.40 = (bf16[48,768]{1,0:T(8,128)(2,1)S(1)}, bf16[48,768]{1,0:T(8,128)(2,1)S(1)}, u32[]{:S(2)}, u32[]{:S(2)}) collective-permute-start(bf16[48,768]{1,0:T(8,128)(2,1)S(1)} %add_convert_fusion.20), channel_id=1, source_target_pairs={{0,8},{4,12},{8,0},{12,4},{16,24},{20,28},{24,16},{28,20},{1,9},{5... | collective-permute-start | bytes 221192 | tf_op jit(solution)/shard_map/ppermute | solution.py:59
  365.1 9.7 %collective-permute-start.48 = (bf16[48,768]{1,0:T(8,128)(2,1)S(1)}, bf16[48,768]{1,0:T(8,128)(2,1)S(1)}, u32[]{:S(2)}, u32[]{:S(2)}) collective-permute-start(bf16[48,768]{1,0:T(8,128)(2,1)S(1)} %add_convert_fusion.15), channel_id=1, source_target_pairs={{0,16},{4,20},{8,24},{12,28},{16,0},{20,4},{24,8},{28,12},{1,17},{... | collective-permute-start | bytes 221192 | tf_op jit(solution)/shard_map/ppermute | solution.py:59
  367.4 9.9 %collective-permute-start.27 = (bf16[48,768]{1,0:T(8,128)(2,1)S(1)}, bf16[48,768]{1,0:T(8,128)(2,1)S(1)}, u32[]{:S(2)}, u32[]{:S(2)}) collective-permute-start(bf16[48,768]{1,0:T(8,128)(2,1)S(1)} %add_convert_fusion.27), channel_id=1, source_target_pairs={{0,16},{4,20},{8,24},{12,28},{16,0},{20,4},{24,8},{28,12},{1,17},{... | collective-permute-start | bytes 221192 | tf_op jit(solution)/shard_map/ppermute | solution.py:59
  369.4 9.0 %collective-permute-start.34 = (bf16[48,768]{1,0:T(8,128)(2,1)S(1)}, bf16[48,768]{1,0:T(8,128)(2,1)S(1)}, u32[]{:S(2)}, u32[]{:S(2)}) collective-permute-start(bf16[48,768]{1,0:T(8,128)(2,1)S(1)} %add_convert_fusion.23), channel_id=1, source_target_pairs={{0,16},{4,20},{8,24},{12,28},{16,0},{20,4},{24,8},{28,12},{1,17},{... | collective-permute-start | bytes 221192 | tf_op jit(solution)/shard_map/ppermute | solution.py:59
  372.2 29.0 %collective-permute-start.59 = (bf16[768,768]{1,0:T(8,128)(2,1)S(1)}, bf16[768,768]{1,0:T(8,128)(2,1)S(1)}, u32[]{:S(2)}, u32[]{:S(2)}) collective-permute-start(bf16[768,768]{1,0:T(8,128)(2,1)S(1)} %fusion.1), channel_id=1, source_target_pairs={{0,2},{1,3},{2,0},{3,1},{4,6},{5,7},{6,4},{7,5},{8,10},{9,11},{10,... | collective-permute-start | bytes 3538952 | tf_op jit(solution)/shard_map/ppermute | solution.py:59
  374.4 47.8 %collective-permute-start.52 = (bf16[192,3072]{1,0:T(8,128)(2,1)S(1)}, bf16[192,3072]{1,0:T(8,128)(2,1)S(1)}, u32[]{:S(2)}, u32[]{:S(2)}) collective-permute-start(bf16[192,3072]{1,0:T(8,128)(2,1)S(1)} %fusion), channel_id=1, source_target_pairs={{0,2},{1,3},{2,0},{3,1},{4,6},{5,7},{6,4},{7,5},{8,10},{9,11},{10,... | collective-permute-start | bytes 3538952 | tf_op jit(solution)/shard_map/ppermute | solution.py:59
  374.8 6.2 %collective-permute-start.41 = (bf16[48,768]{1,0:T(8,128)(2,1)S(1)}, bf16[48,768]{1,0:T(8,128)(2,1)S(1)}, u32[]{:S(2)}, u32[]{:S(2)}) collective-permute-start(bf16[48,768]{1,0:T(8,128)(2,1)S(1)} %add_convert_fusion.19), channel_id=1, source_target_pairs={{0,16},{4,20},{8,24},{12,28},{16,0},{20,4},{24,8},{28,12},{1,17},{... | collective-permute-start | bytes 221192 | tf_op jit(solution)/shard_map/ppermute | solution.py:59
  377.3 5.2 %collective-permute-start.49 = (bf16[48,768]{1,0:T(8,128)(2,1)S(1)}, bf16[48,768]{1,0:T(8,128)(2,1)S(1)}, u32[]{:S(2)}, u32[]{:S(2)}) collective-permute-start(bf16[48,768]{1,0:T(8,128)(2,1)S(1)} %add_convert_fusion.14), channel_id=1, source_target_pairs={{0,8},{4,12},{8,0},{12,4},{16,24},{20,28},{24,16},{28,20},{1,9},{5... | collective-permute-start | bytes 221192 | tf_op jit(solution)/shard_map/ppermute | solution.py:59
  378.4 45.3 %collective-permute-start.28 = (bf16[48,768]{1,0:T(8,128)(2,1)S(1)}, bf16[48,768]{1,0:T(8,128)(2,1)S(1)}, u32[]{:S(2)}, u32[]{:S(2)}) collective-permute-start(bf16[48,768]{1,0:T(8,128)(2,1)S(1)} %add_convert_fusion.26), channel_id=1, source_target_pairs={{0,8},{4,12},{8,0},{12,4},{16,24},{20,28},{24,16},{28,20},{1,9},{5... | collective-permute-start | bytes 221192 | tf_op jit(solution)/shard_map/ppermute | solution.py:59
  381.0 43.9 %collective-permute-start.35 = (bf16[48,768]{1,0:T(8,128)(2,1)S(1)}, bf16[48,768]{1,0:T(8,128)(2,1)S(1)}, u32[]{:S(2)}, u32[]{:S(2)}) collective-permute-start(bf16[48,768]{1,0:T(8,128)(2,1)S(1)} %add_convert_fusion.22), channel_id=1, source_target_pairs={{0,8},{4,12},{8,0},{12,4},{16,24},{20,28},{24,16},{28,20},{1,9},{5... | collective-permute-start | bytes 221192 | tf_op jit(solution)/shard_map/ppermute | solution.py:59
  382.6 43.4 %collective-permute-start.42 = (bf16[48,768]{1,0:T(8,128)(2,1)S(1)}, bf16[48,768]{1,0:T(8,128)(2,1)S(1)}, u32[]{:S(2)}, u32[]{:S(2)}) collective-permute-start(bf16[48,768]{1,0:T(8,128)(2,1)S(1)} %add_convert_fusion.18), channel_id=1, source_target_pairs={{0,8},{4,12},{8,0},{12,4},{16,24},{20,28},{24,16},{28,20},{1,9},{5... | collective-permute-start | bytes 221192 | tf_op jit(solution)/shard_map/ppermute | solution.py:59
  401.2 91.9 %collective-permute-start.50 = (bf16[96,768]{1,0:T(8,128)(2,1)S(1)}, bf16[96,768]{1,0:T(8,128)(2,1)S(1)}, u32[]{:S(2)}, u32[]{:S(2)}) collective-permute-start(bf16[96,768]{1,0:T(8,128)(2,1)S(1)} %maximum_select_fusion.11), channel_id=1, source_target_pairs={{0,4},{4,0},{8,12},{12,8},{16,20},{20,16},{24,28},{28,24},{1,5},{5... | collective-permute-start | bytes 442376 | tf_op jit(solution)/shard_map/ppermute | solution.py:59
  422.2 30.4 %collective-permute-start.60 = (bf16[384,768]{1,0:T(8,128)(2,1)S(1)}, bf16[384,768]{1,0:T(8,128)(2,1)S(1)}, u32[]{:S(2)}, u32[]{:S(2)}) collective-permute-start(bf16[384,768]{1,0:T(8,128)(2,1)S(1)} %get-tuple-element.120), channel_id=1, source_target_pairs={{0,4},{4,0},{8,12},{12,8},{16,20},{20,16},{24,28},{28,24},{1,5},{5... | collective-permute-start | bytes 1769480 | tf_op jit(solution)/shard_map/ppermute | solution.py:59
  423.7 31.0 %collective-permute-start.53 = (bf16[96,3072]{1,0:T(8,128)(2,1)S(1)}, bf16[96,3072]{1,0:T(8,128)(2,1)S(1)}, u32[]{:S(2)}, u32[]{:S(2)}) collective-permute-start(bf16[96,3072]{1,0:T(8,128)(2,1)S(1)} %get-tuple-element.122), channel_id=1, source_target_pairs={{0,4},{4,0},{8,12},{12,8},{16,20},{20,16},{24,28},{28,24},{1,5},{5... | collective-permute-start | bytes 1769480 | tf_op jit(solution)/shard_map/ppermute | solution.py:59
  425.0 27.4 %collective-permute-start.29 = (bf16[96,768]{1,0:T(8,128)(2,1)S(1)}, bf16[96,768]{1,0:T(8,128)(2,1)S(1)}, u32[]{:S(2)}, u32[]{:S(2)}) collective-permute-start(bf16[96,768]{1,0:T(8,128)(2,1)S(1)} %maximum_select_fusion.8), channel_id=1, source_target_pairs={{0,4},{4,0},{8,12},{12,8},{16,20},{20,16},{24,28},{28,24},{1,5},{5... | collective-permute-start | bytes 442376 | tf_op jit(solution)/shard_map/ppermute | solution.py:59
  426.0 47.2 %collective-permute-start.36 = (bf16[96,768]{1,0:T(8,128)(2,1)S(1)}, bf16[96,768]{1,0:T(8,128)(2,1)S(1)}, u32[]{:S(2)}, u32[]{:S(2)}) collective-permute-start(bf16[96,768]{1,0:T(8,128)(2,1)S(1)} %maximum_select_fusion.9), channel_id=1, source_target_pairs={{0,4},{4,0},{8,12},{12,8},{16,20},{20,16},{24,28},{28,24},{1,5},{5... | collective-permute-start | bytes 442376 | tf_op jit(solution)/shard_map/ppermute | solution.py:59
  452.3 31.3 %collective-permute-start.43 = (bf16[96,768]{1,0:T(8,128)(2,1)S(1)}, bf16[96,768]{1,0:T(8,128)(2,1)S(1)}, u32[]{:S(2)}, u32[]{:S(2)}) collective-permute-start(bf16[96,768]{1,0:T(8,128)(2,1)S(1)} %maximum_select_fusion.10), channel_id=1, source_target_pairs={{0,4},{4,0},{8,12},{12,8},{16,20},{20,16},{24,28},{28,24},{1,5},{5... | collective-permute-start | bytes 442376 | tf_op jit(solution)/shard_map/ppermute | solution.py:59
  452.8 9.5 %collective-permute-start.61 = (bf16[192,768]{1,0:T(8,128)(2,1)S(1)}, bf16[192,768]{1,0:T(8,128)(2,1)S(1)}, u32[]{:S(2)}, u32[]{:S(2)}) collective-permute-start(bf16[192,768]{1,0:T(8,128)(2,1)S(1)} %add_convert_fusion.4), channel_id=1, source_target_pairs={{0,8},{4,12},{8,0},{12,4},{16,24},{20,28},{24,16},{28,20},{1,9},{5... | collective-permute-start | bytes 884744 | tf_op jit(solution)/shard_map/ppermute | solution.py:59
  454.9 16.8 %collective-permute-start.54 = (bf16[48,3072]{1,0:T(8,128)(2,1)S(1)}, bf16[48,3072]{1,0:T(8,128)(2,1)S(1)}, u32[]{:S(2)}, u32[]{:S(2)}) collective-permute-start(bf16[48,3072]{1,0:T(8,128)(2,1)S(1)} %add_convert_fusion.8), channel_id=1, source_target_pairs={{0,8},{4,12},{8,0},{12,4},{16,24},{20,28},{24,16},{28,20},{1,9},{5... | collective-permute-start | bytes 884744 | tf_op jit(solution)/shard_map/ppermute | solution.py:59
  462.4 12.5 %collective-permute-start.62 = (bf16[192,768]{1,0:T(8,128)(2,1)S(1)}, bf16[192,768]{1,0:T(8,128)(2,1)S(1)}, u32[]{:S(2)}, u32[]{:S(2)}) collective-permute-start(bf16[192,768]{1,0:T(8,128)(2,1)S(1)} %add_convert_fusion.3), channel_id=1, source_target_pairs={{0,16},{4,20},{8,24},{12,28},{16,0},{20,4},{24,8},{28,12},{1,17},{... | collective-permute-start | bytes 884744 | tf_op jit(solution)/shard_map/ppermute | solution.py:59
  471.8 11.6 %collective-permute-start.55 = (bf16[48,3072]{1,0:T(8,128)(2,1)S(1)}, bf16[48,3072]{1,0:T(8,128)(2,1)S(1)}, u32[]{:S(2)}, u32[]{:S(2)}) collective-permute-start(bf16[48,3072]{1,0:T(8,128)(2,1)S(1)} %add_convert_fusion.7), channel_id=1, source_target_pairs={{0,16},{4,20},{8,24},{12,28},{16,0},{20,4},{24,8},{28,12},{1,17},{... | collective-permute-start | bytes 884744 | tf_op jit(solution)/shard_map/ppermute | solution.py:59
  475.0 10.0 %collective-permute-start.63 = (bf16[192,768]{1,0:T(8,128)(2,1)S(1)}, bf16[192,768]{1,0:T(8,128)(2,1)S(1)}, u32[]{:S(2)}, u32[]{:S(2)}) collective-permute-start(bf16[192,768]{1,0:T(8,128)(2,1)S(1)} %add_convert_fusion.2), channel_id=1, source_target_pairs={{0,8},{4,12},{8,0},{12,4},{16,24},{20,28},{24,16},{28,20},{1,9},{5... | collective-permute-start | bytes 884744 | tf_op jit(solution)/shard_map/ppermute | solution.py:59
  483.5 6.8 %collective-permute-start.56 = (bf16[48,3072]{1,0:T(8,128)(2,1)S(1)}, bf16[48,3072]{1,0:T(8,128)(2,1)S(1)}, u32[]{:S(2)}, u32[]{:S(2)}) collective-permute-start(bf16[48,3072]{1,0:T(8,128)(2,1)S(1)} %add_convert_fusion.6), channel_id=1, source_target_pairs={{0,8},{4,12},{8,0},{12,4},{16,24},{20,28},{24,16},{28,20},{1,9},{5... | collective-permute-start | bytes 884744 | tf_op jit(solution)/shard_map/ppermute | solution.py:59
  485.1 10.4 %collective-permute-start.64 = (bf16[384,768]{1,0:T(8,128)(2,1)S(1)}, bf16[384,768]{1,0:T(8,128)(2,1)S(1)}, u32[]{:S(2)}, u32[]{:S(2)}) collective-permute-start(bf16[384,768]{1,0:T(8,128)(2,1)S(1)} %maximum_select_fusion.3), channel_id=1, source_target_pairs={{0,4},{4,0},{8,12},{12,8},{16,20},{20,16},{24,28},{28,24},{1,5},{5... | collective-permute-start | bytes 1769480 | tf_op jit(solution)/shard_map/ppermute | solution.py:59
  490.4 11.5 %collective-permute-start.57 = (bf16[96,3072]{1,0:T(8,128)(2,1)S(1)}, bf16[96,3072]{1,0:T(8,128)(2,1)S(1)}, u32[]{:S(2)}, u32[]{:S(2)}) collective-permute-start(bf16[96,3072]{1,0:T(8,128)(2,1)S(1)} %maximum_select_fusion.2), channel_id=1, source_target_pairs={{0,4},{4,0},{8,12},{12,8},{16,20},{20,16},{24,28},{28,24},{1,5},{5... | collective-permute-start | bytes 1769480 | tf_op jit(solution)/shard_map/ppermute | solution.py:59
  (57 other events, 672.5 us)
